TPU v7x, 512 devices: a whole 4x4x16 slice. The times are simulated.
512 devices in a mesh: vol: 128 (over z, x, core), rep: 4 (over y).
Axes of the slice: x: 4, y: 4, z: 16, core: 2. Of those that a mesh axis runs over, the one named last changes fastest.
Arguments:
- cutouts: bfloat16 [4, 4096, 4096], P('rep', 'vol'), may hold values from -6 to 6
- counts: int32 [4, 128], P('rep', 'vol'), may hold values from 1 to 32, as said below
- partner: int32 [4, 2048], P('rep'), may hold values from 0 to 2047, as said below
- w_stem: bfloat16 [64, 128], replicated, may hold values from -0.75 to 0.75
- w_mix: bfloat16 [128, 128], replicated, may hold values from -0.5 to 0.5
- w_out: bfloat16 [128, 128], replicated, may hold values from -0.5 to 0.5
- w_proj: bfloat16 [128, 64], replicated, may hold values from -0.5 to 0.5
Outputs:
- upd_stem: float32 [64, 128], replicated
- upd_mix: float32 [128, 128], replicated
- upd_out: float32 [128, 128], replicated
- upd_proj: float32 [128, 64], replicated
- node_loss: float32 [4, 128, 16], P('rep', 'vol')
Inputs may be any that keep to these rules, and one draw needn't show every extreme that they name: `counts`: each row sums to 2048, and its largest entry is exactly 32. Each row pairs the nodes of a group: partner[r, partner[r, g]] = g and partner[r, g] != g.
All inputs are finite; a program needn't handle non-finite values.
Results may differ from a plain program's by a relative error of at most 0.0035.
Values may be sent and summed in bfloat16 or wider, within the bound.
A program may use at most 64 MiB of HBM per device.

v0:
```python
import jax
import jax.numpy as jnp
from jax import lax
from jax.sharding import PartitionSpec as P

logit_divisor_factor = 0.2
norm_eps = 1e-06
rms_eps = 1e-06


def prefix(part, axis, combine, identity):
    place = lax.axis_index(axis)
    gathered = lax.all_gather(part, axis)
    state = jnp.zeros_like(part) + jnp.asarray(identity, part.dtype)

    def one(lap, state):
        return combine(state, lax.dynamic_index_in_dim(gathered, lap, 0, False))

    return lax.fori_loop(0, place, one, state)


def first_dot(left, right):
    return lax.dot_general(
        left, right, (((0,), (0,)), ((), ())), preferred_element_type=jnp.float32
    )


def concluding_matrix_multiply(left, right):
    return lax.dot_general(
        left, right, (((1,), (1,)), ((), ())), preferred_element_type=jnp.float32
    )


def silu_slope(value):
    sigma = jax.nn.sigmoid(value)
    return sigma * (1.0 + value * (1.0 - sigma))


def encode(cutout_rows, w_stem, w_mix, w_out, w_proj):
    number = cutout_rows.shape[0]
    patches = cutout_rows.reshape(-1, w_stem.shape[0])
    per_cutout = patches.shape[0] // number
    pre_stem = jnp.dot(patches, w_stem, preferred_element_type=jnp.float32)
    hidden = jax.nn.silu(pre_stem).astype(jnp.bfloat16)
    pre_mix = jnp.dot(hidden, w_mix, preferred_element_type=jnp.float32)
    mixed = jax.nn.silu(pre_mix).astype(jnp.bfloat16)
    summed = hidden.astype(jnp.float32) + jnp.dot(mixed, w_out, preferred_element_type=jnp.float32)
    pooled = jnp.mean(summed.reshape(number, per_cutout, -1), axis=1).astype(jnp.bfloat16)
    raw_embed = jnp.dot(pooled, w_proj, preferred_element_type=jnp.float32)
    inv_norm = lax.rsqrt(jnp.sum(raw_embed * raw_embed, axis=1, keepdims=True) + norm_eps)
    unit_embed = raw_embed * inv_norm
    return (unit_embed, (patches, pre_stem, hidden, pre_mix, mixed, pooled, unit_embed, inv_norm))


def backward(feature_vector_derivative, saved, w_mix, w_out, w_proj):
    patches, pre_stem, hidden, pre_mix, mixed, pooled, unit_embed, inv_norm = saved
    number = pooled.shape[0]
    per_cutout = patches.shape[0] // number
    channels = hidden.shape[1]
    radial = jnp.sum(unit_embed * feature_vector_derivative, axis=1, keepdims=True)
    grad_raw = (inv_norm * (feature_vector_derivative - unit_embed * radial)).astype(jnp.bfloat16)
    grad_proj = first_dot(pooled, grad_raw)
    grad_pool = (concluding_matrix_multiply(grad_raw, w_proj) / per_cutout).astype(jnp.bfloat16)
    mixed_sum = jnp.sum(mixed.reshape(number, per_cutout, channels), axis=1, dtype=jnp.float32)
    grad_out = lax.dot_general(
        mixed_sum,
        grad_pool.astype(jnp.float32),
        (((0,), (0,)), ((), ())),
        precision=lax.Precision.HIGHEST,
        preferred_element_type=jnp.float32,
    )
    grad_mixed = concluding_matrix_multiply(grad_pool, w_out)
    mix_slope = silu_slope(pre_mix).reshape(number, per_cutout, channels)
    grad_pre_mix = (grad_mixed[:, None, :] * mix_slope).reshape(-1, channels).astype(jnp.bfloat16)
    grad_mix = first_dot(hidden, grad_pre_mix)
    spread_pool = jnp.broadcast_to(
        grad_pool.astype(jnp.float32)[:, None, :], (number, per_cutout, channels)
    ).reshape(-1, channels)
    grad_hidden = spread_pool + concluding_matrix_multiply(grad_pre_mix, w_mix)
    grad_pre_stem = (grad_hidden * silu_slope(pre_stem)).astype(jnp.bfloat16)
    grad_stem = first_dot(patches, grad_pre_stem)
    return (grad_stem, grad_mix, grad_out, grad_proj)


def contrast(anchor_feature_matrix, whole_feature_matrix, self_pos, pair_pos):
    cosine_affinity_matrix = (
        concluding_matrix_multiply(anchor_feature_matrix, whole_feature_matrix)
        / logit_divisor_factor
    )
    columns = lax.broadcasted_iota(jnp.int32, cosine_affinity_matrix.shape, 1)
    exp_scores = jnp.where(columns == self_pos[:, None], 0.0, jnp.exp(cosine_affinity_matrix))
    log_total = jnp.log(jnp.sum(exp_scores, axis=1))
    companion_feature_vector = jnp.take(whole_feature_matrix, pair_pos, axis=0).astype(jnp.float32)
    positive_couple_affinity = (
        jnp.sum(anchor_feature_matrix.astype(jnp.float32) * companion_feature_vector, axis=1)
        / logit_divisor_factor
    )
    return (exp_scores, log_total, companion_feature_vector, log_total - positive_couple_affinity)


def add_counts(earlier, later):
    return earlier + later


def locate(recv_ids, node_rank, slot_index):
    matches = recv_ids[None, :] == node_rank[:, None]
    from_slot = jnp.sum(jnp.where(matches, slot_index[None, :], 0), axis=1)
    return (matches, from_slot)


def on_device(cutouts, counts, partner, w_stem, w_mix, w_out, w_proj):
    vol_size = lax.axis_size("vol")
    vol_index = lax.axis_index("vol")
    max_nodes = cutouts.shape[1]
    node_dev = partner.shape[1] // vol_size
    capacity = (max_nodes + vol_size - 1) // vol_size
    own_cutouts = cutouts[0]
    own_count = counts[0, 0]
    offset = prefix(counts, "vol", add_counts, jnp.zeros_like(counts))[0, 0]
    slot_index = jnp.arange(vol_size * capacity, dtype=jnp.int32)
    target = slot_index // capacity
    first_rank = (offset - target + vol_size - 1) // vol_size
    slot_rank = first_rank + slot_index % capacity
    local_slot = slot_rank * vol_size + target - offset
    is_live = local_slot < own_count
    local_safe = jnp.clip(local_slot, 0, max_nodes - 1)
    send_ids = jnp.where(is_live, slot_rank, -1).astype(jnp.int32)
    node_rank = jnp.arange(node_dev, dtype=jnp.int32)
    packed = jnp.where(
        is_live[:, None], jnp.take(own_cutouts, local_safe, axis=0), jnp.zeros((), jnp.bfloat16)
    )
    arrived, recv_ids = (
        lax.all_to_all(packed, "vol", split_axis=0, concat_axis=0, tiled=True),
        lax.all_to_all(send_ids, "vol", split_axis=0, concat_axis=0, tiled=True),
    )
    matches, from_slot = locate(recv_ids, node_rank, slot_index)
    unit_embed, saved = encode(jnp.take(arrived, from_slot, axis=0), w_stem, w_mix, w_out, w_proj)
    anchor_feature_matrix = unit_embed.astype(jnp.bfloat16)
    whole_feature_matrix = lax.all_gather(anchor_feature_matrix, "vol", axis=0, tiled=True)
    self_pos = vol_index * node_dev + node_rank
    node_global = node_rank * vol_size + vol_index
    pair_global = jnp.take(partner[0], node_global)
    pair_pos = pair_global % vol_size * node_dev + pair_global // vol_size
    exp_scores, log_total, companion_feature_vector, node_loss = contrast(
        anchor_feature_matrix, whole_feature_matrix, self_pos, pair_pos
    )
    row_weight = (exp_scores * jnp.exp(-log_total)[:, None]).astype(jnp.bfloat16)
    horizontal_objective_term = jnp.dot(
        row_weight, whole_feature_matrix, preferred_element_type=jnp.float32
    )
    all_totals = lax.all_gather(log_total, "vol", axis=0, tiled=True)
    column_weight = (exp_scores * jnp.exp(-all_totals)[None, :]).astype(jnp.bfloat16)
    vertical_objective_term = jnp.dot(
        column_weight, whole_feature_matrix, preferred_element_type=jnp.float32
    )
    feature_vector_derivative = (
        horizontal_objective_term + vertical_objective_term - 2.0 * companion_feature_vector
    ) / logit_divisor_factor
    grads = backward(feature_vector_derivative, saved, w_mix, w_out, w_proj)
    grad_totals = lax.psum((grads[0], grads[1], grads[2], grads[3]), ("vol", "rep"))
    updates = [
        summed_grad * lax.rsqrt(jnp.mean(summed_grad * summed_grad) + rms_eps)
        for summed_grad in grad_totals
    ]
    return (updates[0], updates[1], updates[2], updates[3], node_loss[None, None, :])


def solution(mesh):
    in_specs = (P("rep", "vol", None), P("rep", "vol"), P("rep", None), P(), P(), P(), P())
    out_specs = (P(), P(), P(), P(), P("rep", "vol", None))
    return jax.shard_map(
        on_device, mesh=mesh, in_specs=in_specs, out_specs=out_specs, check_vma=False
    )
```

profile of v0, /device:TPU:1, one launch (start us, length us, event | category | flops | bytes accessed | tf_op | source)
XLA Modules:
  0.0 1521.7 jit_solution(11916330681556625785)
XLA Ops:
  7.2 0.0 copy-start
  7.9 1.3 dynamic-slice
  9.1 0.7 bitcast_dynamic-update-slice_fusion
  9.8 30.3 %all-reduce = s32[128]{0:T(128)S(1)} all-reduce(s32[128]{0:T(128)S(1)} %bitcast_dynamic-update-slice_fusion), channel_id=2, replica_groups=mesh['vol'=128,'rep'=4] {'vol'}, use_global_device_ids=true, to_apply=%add | all-reduce | flops 128 | bytes 1024
  40.1 1.2 while.10
  40.1 0.6 constant_dynamic-slice_fusion.2
  41.4 1.0 compare_select_fusion
  42.4 165.0 %all-to-all-start = ((s32[128,1,1]{2,1,0:T(1,128)}), s32[128,1,1]{2,1,0:T(1,128)S(1)}, u32[]{:S(2)}, u32[]{:S(2)}) async-start(s32[128,1,1]{2,1,0:T(1,128)} %compare_select_fusion), calls=%async_computation | async-start | bytes 131072 | tf_op jit(solution)/shard_map/all_to_all | solution.py:134
  207.5 1.2 gather_fusion
  208.7 0.2 fusion.8
  208.9 0.5 broadcast.861
  209.4 1.4 reduce.1
  210.8 0.0 copy-start.1
  210.8 1.6 reshape.467
  212.4 9.8 all-to-all-done
  222.2 6.3 all-to-all-start.1
  228.6 0.0 all-reduce.7.cloned.1.call-start
  229.3 0.7 gather_fusion.2
  230.0 2.4 reduce
  232.4 0.1 select_reduce_fusion
  232.5 0.1 broadcast_in_dim.85
  232.6 0.1 broadcast_in_dim.86
  232.7 47.7 %all-to-all-done.1 = bf16[128,2,2048]{2,1,0:T(2,128)(2,1)S(1)} async-done(((bf16[128,2,2048]{2,1,0:T(2,128)(2,1)}), bf16[128,2,2048]{2,1,0:T(2,128)(2,1)S(1)}, u32[]{:S(2)}, u32[]{:S(2)}) %all-to-all-start.1) | async-done | bytes 1048608 | tf_op jit(solution)/shard_map/all_to_all | solution.py:133
  280.4 1.0 reshape.468
  281.5 1.1 copy.23
  282.6 0.0 copy-start.4
  282.6 0.6 gather_fusion.1
  283.3 0.2 gather.25
  283.5 0.9 multiply_convert_fusion.1
  284.5 0.0 copy-start.2
  284.5 0.3 convert_reduce_fusion
  284.8 0.2 bitcast_reduce_fusion
  285.1 0.1 copy-done.2
  285.2 0.2 multiply_reduce_fusion.5
  285.5 0.1 multiply_convert_fusion.8
  285.5 85.6 %all_gather.14 = bf16[2048,64]{1,0:T(8,128)(2,1)S(1)} all-gather(bf16[16,64]{1,0:T(8,128)(2,1)S(1)} %multiply_convert_fusion.8), channel_id=1, replica_groups=mesh['vol'=128,'rep'=4] {'vol'}, dimensions={0}, use_global_device_ids=true | all-gather | bytes 264192 | tf_op jit(solution)/shard_map/all_gather | solution.py:139
  371.1 0.6 gather_fusion.3
  371.7 0.4 fusion.35
  372.1 0.2 fusion.19
  372.3 0.6 subtract_bitcast_fusion
  372.8 250.4 %all-reduce.1 = f32[2048]{0:T(1024)S(1)} all-reduce(f32[2048]{0:T(1024)S(1)} %get-tuple-element.64), channel_id=1, replica_groups=mesh['vol'=128,'rep'=4] {'vol'}, use_global_device_ids=true, to_apply=%add.1 | all-reduce | flops 2048 | bytes 16384
  623.2 0.2 fusion.16
  623.4 0.3 multiply_reduce_fusion.4
  623.8 0.1 multiply_convert_fusion.6
  623.8 0.8 fusion.20
  624.7 0.1 fusion.7
  624.8 0.1 fusion.36
  624.9 0.2 fusion.9
  625.1 0.9 fusion.37
  626.1 1.1 fusion.4
  627.2 0.0 all-reduce.7.cloned.1.call-update
  627.2 0.0 all-reduce.9.cloned.1.call-start
  627.3 0.9 fusion.38
  628.1 0.0 all-reduce.9.cloned.1.call-update
  628.2 432.2 %all-reduce.7.cloned.1.call-done = (f32[64,128]{1,0:T(8,128)}, f32[128,64]{0,1:T(8,128)}) async-done(((f32[64,128]{1,0:T(8,128)}, f32[128,64]{0,1:T(8,128)}), (f32[64,128]{1,0:T(8,128)}, f32[128,64]{0,1:T(8,128)})) %all-reduce.7.cloned.1.call-update) | async-done | bytes 65552 | tf_op jit(solution)/shard_map/psum | solution.py:160
  1060.3 1.4 multiply_reduce_fusion.2
  1062.4 1.4 broadcast_multiply_fusion.2
  1063.8 1.4 multiply_reduce_fusion.3
  1065.8 1.4 broadcast_multiply_fusion.3
  1067.2 440.3 %all-reduce.9.cloned.1.call-done = (f32[128,128]{1,0:T(8,128)}, f32[128,128]{1,0:T(8,128)}) async-done(((f32[128,128]{1,0:T(8,128)}, f32[128,128]{1,0:T(8,128)}), (f32[128,128]{1,0:T(8,128)}, f32[128,128]{1,0:T(8,128)})) %all-reduce.9.cloned.1.call-update) | async-done | bytes 131088 | tf_op jit(solution)/shard_map/psum | solution.py:160
  1507.6 1.5 multiply_reduce_fusion
  1509.7 1.5 broadcast_multiply_fusion
  1511.2 1.5 multiply_reduce_fusion.1
  1513.3 1.5 broadcast_multiply_fusion.1
  (24 shorter events, 0.2 us)
Async XLA Ops:
  7.2 200.3 %copy-start = (bf16[1,32,4096]{2,1,0:T(8,128)(2,1)S(1)}, bf16[1,32,4096]{2,1,0:T(8,128)(2,1)}, u32[]{:S(2)}) copy-start(bf16[1,32,4096]{2,1,0:T(8,128)(2,1)} %param.9) | copy-start | bytes 786436
  42.4 179.8 %all-to-all-start = ((s32[128,1,1]{2,1,0:T(1,128)}), s32[128,1,1]{2,1,0:T(1,128)S(1)}, u32[]{:S(2)}, u32[]{:S(2)}) async-start(s32[128,1,1]{2,1,0:T(1,128)} %compare_select_fusion), calls=%async_computation | async-start | bytes 131072 | tf_op jit(solution)/shard_map/all_to_all | solution.py:134
  210.8 18.5 %copy-start.1 = (s32[1,2048]{1,0:T(1,128)S(1)}, s32[1,2048]{1,0:T(1,128)}, u32[]{:S(2)}) copy-start(s32[1,2048]{1,0:T(1,128)} %param.11) | copy-start | bytes 24580
  222.2 58.2 %all-to-all-start.1 = ((bf16[128,2,2048]{2,1,0:T(2,128)(2,1)}), bf16[128,2,2048]{2,1,0:T(2,128)(2,1)S(1)}, u32[]{:S(2)}, u32[]{:S(2)}) async-start(bf16[128,2,2048]{2,1,0:T(2,128)(2,1)} %reshape.467), calls=%async_computation.1 | async-start | bytes 2097152 | tf_op jit(solution)/shard_map/all_to_all | solution.py:133
  228.6 831.8 %all-reduce.7.cloned.1.call-start = ((), (), s32[]{:S(2)}) async-start(), calls=%async_computation.2 | async-start | bytes 131072 | tf_op jit(solution)/shard_map/psum | solution.py:160
  281.5 2.1 copy-start.5
  282.6 1.9 copy-start.4
  283.5 1.3 copy-start.3
  284.5 0.7 copy-start.2
  627.2 880.3 %all-reduce.9.cloned.1.call-start = ((), (), s32[]{:S(2)}) async-start(), calls=%async_computation.3 | async-start | bytes 262144 | tf_op jit(solution)/shard_map/psum | solution.py:160
Sparse Core Ops, SparseCore 0:
  627.3 432.9 all-reduce.6
  1067.4 440.1 all-reduce.8
where the time goes:
time: 1530 us; the launch traced here: 1520 us
  waiting for transfers between devices  930 us (61%)
  blocking collectives  366 us (24%)
  starting transfers between devices  171 us (11%)
  between operations  18.5 us (1%)
  other arithmetic  17.8 us (1%)
    psum x2, waiting for transfers between devices, on_device(): lax.psum((grads[0], grads[1], grads[2], grads[3]), ('vol', 'rep'))  873 us
    unnamed x2, blocking collectives  281 us
    all_to_all x1, starting transfers between devices, on_device(): lax.all_to_all(send_ids, 'vol', split_axis=0, concat_axis=0, tiled=True)  165 us
    all_gather x1, blocking collectives, on_device(): lax.all_gather(anchor_feature_matrix, 'vol', axis=0, tiled=True)  85.6 us
    all_to_all x1, waiting for transfers between devices, on_device(): lax.all_to_all(packed, 'vol', split_axis=0, concat_axis=0, tiled=True)  47.7 us
  transfers between devices with their start and end apart: 4, of which 4 were waited for; matrix products, arithmetic and copies ran while one was open for 1% of the time, Pallas kernels for 0%

commit v1 on v0

v1 whole, which is shorter than its diff:
```python
import functools

import jax
import jax.numpy as jnp
from jax import lax
from jax.experimental import pallas as pl
from jax.experimental.pallas import tpu as pltpu
from jax.sharding import PartitionSpec as P

MESH = pl.DeviceIdType.MESH
F32 = jnp.float32
BF16 = jnp.bfloat16
HIGHEST = lax.Precision.HIGHEST

NZ, NP, NY = 16, 8, 4
NV = NZ * NP
NQ = NP * NY
C, E, VOX, PATCHES = 128, 64, 64, 64
SLOTS, HALF = 32, 16
NODES = 2048
DEAD = NV * SLOTS - NODES
NEAR = 4
PAIRS = PATCHES // 2
ROWS = PAIRS * SLOTS
CHUNK = 256
LINE = NZ * HALF
TEMPERATURE = 0.2
LOG2E = 1.4426950408889634
SCALE = LOG2E / TEMPERATURE
EPS = 1e-6


def iota(shape, dim):
    return lax.broadcasted_iota(jnp.int32, shape, dim)


def dot(a, b, precision=None):
    return lax.dot_general(a, b, (((1,), (0,)), ((), ())), precision=precision, preferred_element_type=F32)


def dot_nt(a, b):
    return lax.dot_general(a, b, (((1,), (1,)), ((), ())), preferred_element_type=F32)


def dot_tn(a, b, precision=None):
    return lax.dot_general(a, b, (((0,), (0,)), ((), ())), precision=precision, preferred_element_type=F32)


def sigmoid(v):
    return 1.0 / (1.0 + jnp.exp(-v))


def twice(v):
    return jnp.concatenate([v, v], axis=1)


def fold(v):
    half = v.shape[1] // 2
    return v[:, :half] + v[:, half:]


def block_diagonal(w):
    zero = jnp.zeros_like(w)
    return jnp.concatenate(
        [jnp.concatenate([w, zero], axis=1), jnp.concatenate([zero, w], axis=1)], axis=0
    )


def kernel(
    cut_ref, count_ref, partner_ref, stem_ref, mix_ref, out_ref, proj_ref,
    up_stem_ref, up_mix_ref, up_out_ref, up_proj_ref, loss_ref,
    x_s, hid_s, slope1_s, slope2_s, xt_s, ht_s,
    emb_s, cnt_s, tot_s, part_s, gath_s, zed_s, fin_s,
    send_sem, recv_sem,
):
    vol = lax.axis_index("vol")
    rep = lax.axis_index("rep")
    z = vol // NP
    p = lax.rem(vol, NP)
    q = rep * NP + p

    def z_peer(step):
        return (lax.rem(z + step + NZ, NZ) * NP + p, rep)

    def p_peer(step):
        return (z * NP + lax.rem(p + step, NP), rep)

    def q_peer(other):
        return (z * NP + lax.rem(other, NP), other // NP)

    def send(src, dst, kind, device):
        pltpu.make_async_remote_copy(
            src_ref=src, dst_ref=dst, send_sem=send_sem.at[kind], recv_sem=recv_sem.at[kind],
            device_id=device, device_id_type=MESH,
        ).start()

    def arrived(ref, kind):
        pltpu.make_async_copy(ref, ref, recv_sem.at[kind]).wait()

    def sent(ref, kind):
        pltpu.make_async_copy(ref, ref, send_sem.at[kind]).wait()

    barrier = pltpu.get_barrier_semaphore()
    greeted = 0
    for step in range(NEAR, 0, -1):
        for sign in (1, -1):
            pl.semaphore_signal(barrier, inc=1, device_id=z_peer(sign * step), device_id_type=MESH)
            greeted += 1
    for step in range(1, NY):
        pl.semaphore_signal(
            barrier, inc=1, device_id=(vol, lax.rem(rep + step, NY)), device_id_type=MESH
        )
        greeted += 1
    for step in range(1, NP):
        pl.semaphore_signal(barrier, inc=1, device_id=p_peer(step), device_id_type=MESH)
        greeted += 1

    count = count_ref[0, 0]
    cnt_s[p, NEAR] = jnp.full((1, 128), count, jnp.int32).astype(F32)
    w_stem2 = block_diagonal(stem_ref[...])
    w_mix2 = block_diagonal(mix_ref[...])
    for pair in range(PAIRS):
        x_s[pair * SLOTS:(pair + 1) * SLOTS, :] = cut_ref[:, pair * 128:(pair + 1) * 128]

    def forward(step, sums):
        hid_sum, mix_sum = sums
        rows = pl.ds(pl.multiple_of(step * CHUNK, CHUNK), CHUNK)
        pre1 = dot(x_s[rows, :], w_stem2)
        sig1 = sigmoid(pre1)
        hidden = (pre1 * sig1).astype(BF16)
        slope1_s[rows, :] = sig1 * (1.0 + pre1 * (1.0 - sig1))
        hid_s[rows, :] = hidden
        pre2 = dot(hidden, w_mix2)
        sig2 = sigmoid(pre2)
        mixed = (pre2 * sig2).astype(BF16)
        slope2_s[rows, :] = sig2 * (1.0 + pre2 * (1.0 - sig2))
        hid_sum = hid_sum + jnp.sum(hidden.astype(F32).reshape(CHUNK // SLOTS, SLOTS, 2 * C), axis=0)
        mix_sum = mix_sum + jnp.sum(mixed.astype(F32).reshape(CHUNK // SLOTS, SLOTS, 2 * C), axis=0)
        return hid_sum, mix_sum

    start = jnp.zeros((SLOTS, 2 * C), F32)
    hid_sum, mix_sum = lax.fori_loop(0, ROWS // CHUNK, forward, (start, start))
    hid_sum, mix_sum = fold(hid_sum), fold(mix_sum)
    w_out = out_ref[...]
    pooled = ((hid_sum + dot(mix_sum, w_out.astype(F32), HIGHEST)) * (1.0 / PATCHES)).astype(BF16)
    raw = dot(pooled, proj_ref[...])
    inv_norm = lax.rsqrt(jnp.sum(raw * raw, axis=1, keepdims=True) + EPS)
    unit = raw * inv_norm
    live = iota((SLOTS, E), 0) < count
    embed = jnp.where(live, unit, 0.0).astype(BF16)
    emb_s[p, NEAR] = jnp.concatenate([embed[:HALF], embed[HALF:]], axis=1)

    pl.semaphore_wait(barrier, greeted)

    own = emb_s.at[p, NEAR]
    own_count = cnt_s.at[p, NEAR]
    for step in range(NEAR, 0, -1):
        for sign in (1, -1):
            send(own, emb_s.at[p, NEAR - sign * step], 0, z_peer(sign * step))
    for step in range(NEAR, 0, -1):
        for sign in (1, -1):
            send(own_count, cnt_s.at[p, NEAR - sign * step], 1, z_peer(sign * step))

    xt_s[...] = x_s[...].T
    ht_s[...] = hid_s[...].T
    lane = iota((HALF, 128), 1)
    zero_half = jnp.zeros((HALF, E), BF16)
    zero_slots = jnp.zeros((SLOTS, E), BF16)
    anchors = jnp.concatenate(
        [jnp.concatenate([embed, zero_slots], axis=1), jnp.concatenate([zero_slots, embed], axis=1)], axis=0
    )

    arrived(emb_s.at[0, 0:2 * NEAR], 0)
    far = NZ - 2 * NEAR - 1
    send(emb_s.at[p, NEAR + 1:2 * NEAR + 1], emb_s.at[p, 2 * NEAR + 1:3 * NEAR + 1], 2, z_peer(-NEAR))
    send(emb_s.at[p, 1:NEAR], emb_s.at[p, 3 * NEAR + 1:4 * NEAR], 2, z_peer(NEAR))
    arrived(cnt_s.at[0, 0:2 * NEAR], 1)
    send(cnt_s.at[p, NEAR + 1:2 * NEAR + 1], cnt_s.at[p, 2 * NEAR + 1:3 * NEAR + 1], 3, z_peer(-NEAR))
    send(cnt_s.at[p, 1:NEAR], cnt_s.at[p, 3 * NEAR + 1:4 * NEAR], 3, z_peer(NEAR))
    near_block = emb_s.at[p, 0:2 * NEAR + 1]
    for step in range(1, NP):
        send(near_block, near_block, 4, p_peer(step))
    arrived(emb_s.at[0, 0:far], 2)
    far_block = emb_s.at[p, 2 * NEAR + 1:NZ]
    for step in range(1, NP):
        send(far_block, far_block, 5, p_peer(step))
    arrived(cnt_s.at[0, 0:far], 3)
    count_block = cnt_s.at[p]
    for step in range(1, NP):
        send(count_block, count_block, 6, p_peer(step))

    line = emb_s[p].reshape(LINE, 128)
    low = iota((LINE, 128), 1) < E
    turned = jnp.concatenate([line[:, E:], line[:, :E]], axis=1)
    none = jnp.zeros_like(line)
    columns = jnp.concatenate(
        [
            jnp.where(low, line, none), jnp.where(low, turned, none),
            jnp.where(low, none, turned), jnp.where(low, none, line),
        ],
        axis=0,
    )

    def scores(part):
        block = emb_s[part].reshape(LINE, 128)
        return jnp.exp2(dot_nt(block, columns) * SCALE)

    def add_rows(e):
        return jnp.sum(e.reshape(LINE // 8, 8, 4 * LINE), axis=0)

    col = iota((LINE, 4 * LINE), 1)
    row = iota((LINE, 4 * LINE), 0)
    self_score = (col == row) | (col == row + 3 * LINE)
    total = add_rows(jnp.where(self_score, 0.0, scores(p)))
    arrived(emb_s.at[0:NP - 1, 0:2 * NEAR + 1], 4)
    arrived(emb_s.at[0:NP - 1, 0:far], 5)

    def other(step, total):
        return total + add_rows(scores(lax.rem(p + step, NP)))

    total = lax.fori_loop(1, NP, other, total)
    line_sum = fold(jnp.sum(total, axis=0, keepdims=True)) - float(DEAD)
    tot_s[p] = jnp.concatenate([line_sum[:, :LINE], line_sum[:, LINE:]], axis=0)
    own_total = tot_s.at[p]
    for step in range(1, NP):
        send(own_total, own_total, 7, p_peer(step))

    every = emb_s[...].reshape(NP * LINE, 128)
    wide = NP * LINE
    exps = jnp.exp2(dot_nt(anchors, every) * SCALE)
    row = iota((2 * SLOTS, wide), 0)
    col = iota((2 * SLOTS, wide), 1)
    slot = lax.rem(row, SLOTS)
    self_score = (row // SLOTS == slot // HALF) & (col == p * LINE + NEAR * HALF + lax.rem(slot, HALF))
    exps = jnp.where(self_score, 0.0, exps)
    row_sum = jnp.sum(exps, axis=1, keepdims=True)
    own_sum = row_sum[:SLOTS] + row_sum[SLOTS:] - float(DEAD)
    own_inv = 1.0 / own_sum
    row_weight = (exps * jnp.concatenate([own_inv, own_inv], axis=0)).astype(BF16)

    arrived(cnt_s.at[0:NP - 1], 6)
    counts = cnt_s[...]
    by_plane = jnp.sum(counts, axis=0)

    def place(relative):
        return lax.rem(z + relative + NZ - NEAR, NZ)

    plane_row = place(iota((NZ, 1, 128), 0))
    numbers = [[], []]
    own_offset = jnp.sum(jnp.where(plane_row < z, by_plane, 0.0), axis=0)
    before = [own_offset]
    for group in range(2):
        relative = iota((NZ, 1, 128), 2) // HALF + group * (NZ // 2)
        offset = jnp.sum(jnp.where(plane_row < place(relative), by_plane, 0.0), axis=0)
        inside = lax.rem(iota((1, 128), 1), HALF).astype(F32)
        for part in range(NP):
            amount = jnp.sum(jnp.where(iota((NZ, 1, 128), 0) == relative, counts[part], 0.0), axis=0)
            for half in range(2):
                position = inside + float(half * HALF)
                numbers[half].append((part, group, jnp.where(position < amount, offset + position, -1.0)))
            offset = offset + amount
    for part in range(NP):
        own_offset = own_offset + jnp.where(part < p, counts[part, NEAR], 0.0)
    number = []
    for half in range(2):
        ordered = sorted(numbers[half], key=lambda item: item[:2])
        number.append(jnp.concatenate([value for _, _, value in ordered], axis=1))

    table = partner_ref[...].astype(F32)
    node = iota((1, NODES), 1).astype(F32)
    own_number = own_offset[:, :1] + iota((SLOTS, 1), 0).astype(F32)
    out_number = (iota((HALF, 1), 0) * NV + vol).astype(F32)
    wanted = jnp.concatenate([own_number, out_number], axis=0)
    mates = jnp.sum(jnp.where(node == wanted, table, 0.0), axis=1, keepdims=True)
    pick = jnp.concatenate([mates, out_number], axis=0)
    picked = [(number[half] == pick) for half in range(2)]
    ones = [jnp.where(match, 1.0, 0.0).astype(BF16) for match in picked]
    first = dot(jnp.concatenate([row_weight] + ones, axis=0), every)
    rows_term = first[:SLOTS, :E] + first[SLOTS:2 * SLOTS, E:]
    n_pick = SLOTS + 2 * HALF
    chosen = first[2 * SLOTS:2 * SLOTS + n_pick, :E] + first[2 * SLOTS + n_pick:, E:]
    companion = chosen[:SLOTS]

    arrived(tot_s.at[0:NP - 1], 7)
    sums = [
        jnp.concatenate([tot_s[part, half:half + 1, :] for part in range(NP)], axis=1) for half in range(2)
    ]
    col_weight = jnp.concatenate(
        [exps[half * SLOTS:(half + 1) * SLOTS] * (1.0 / sums[half]) for half in range(2)], axis=0
    ).astype(BF16)
    second = dot(col_weight, every)
    cols_term = second[:SLOTS, :E] + second[SLOTS:, E:]

    d_embed = (rows_term + cols_term - 2.0 * companion) * (1.0 / TEMPERATURE)
    radial = jnp.sum(unit * d_embed, axis=1, keepdims=True)
    d_raw = jnp.where(live, inv_norm * (d_embed - unit * radial), 0.0).astype(BF16)
    g_proj = dot_tn(d_raw, pooled)
    d_sum = (dot_nt(d_raw, proj_ref[...]) * (1.0 / PATCHES)).astype(BF16)
    d_sum32 = d_sum.astype(F32)
    g_out = dot_tn(mix_sum, d_sum32, HIGHEST)
    d_mixed = twice(dot_nt(d_sum, w_out))
    d_spread = twice(d_sum32)

    for tile in range(NP * 2):
        part_s[16 + tile, 0:8, :] = g_out[tile * 8:(tile + 1) * 8]
        part_s[16 + tile, 8:12, :] = g_proj[tile * 4:(tile + 1) * 4]

    g_mix = jnp.zeros((2 * C, 2 * C), F32)
    g_stem = jnp.zeros((2 * VOX, 2 * C), F32)
    for step in range(ROWS // CHUNK):
        rows = slice(step * CHUNK, (step + 1) * CHUNK)
        shape = (CHUNK // SLOTS, SLOTS, 2 * C)
        d_pre2 = (slope2_s[rows, :].reshape(shape) * d_mixed[None]).reshape(CHUNK, 2 * C).astype(BF16)
        g_mix = g_mix + dot(ht_s[:, rows], d_pre2)
        d_hid = (dot_nt(d_pre2, w_mix2).reshape(shape) + d_spread[None]).reshape(CHUNK, 2 * C)
        d_pre1 = (d_hid * slope1_s[rows, :]).astype(BF16)
        g_stem = g_stem + dot(xt_s[:, rows], d_pre1)
    g_mix = g_mix[:C, :C] + g_mix[C:, C:]
    g_stem = g_stem[:VOX, :C] + g_stem[VOX:, C:]
    for tile in range(NP * 2):
        part_s[tile, 0:8, :] = g_mix[tile * 8:(tile + 1) * 8]
        part_s[tile, 8:12, :] = g_stem[tile * 4:(tile + 1) * 4]

    def scatter(step, carry):
        to = lax.rem(q + step, NQ)
        send(part_s.at[to], gath_s.at[q], 8, q_peer(to))
        return carry

    lax.fori_loop(1, NQ, scatter, 0)
    gath_s[q] = part_s[q]

    out_sum = jnp.zeros((HALF, 1), F32)
    for half in range(2):
        hit = picked[half][SLOTS + HALF:]
        out_sum = out_sum + jnp.sum(jnp.where(hit, sums[half], 0.0), axis=1, keepdims=True)
    affinity = jnp.sum(chosen[SLOTS:SLOTS + HALF] * chosen[SLOTS + HALF:], axis=1, keepdims=True)
    loss = jnp.log(out_sum) - affinity * (1.0 / TEMPERATURE)
    square = iota((HALF, HALF), 0) == iota((HALF, HALF), 1)
    loss_ref[...] = jnp.sum(jnp.where(square, loss, 0.0), axis=0, keepdims=True)

    arrived(gath_s.at[0:NQ - 1], 8)
    zed_s[z] = jnp.sum(gath_s[...], axis=0)
    for step in range(NZ // 2, 0, -1):
        for sign in (1, -1):
            if step < NZ // 2 or sign == 1:
                send(zed_s.at[z], zed_s.at[z], 9, z_peer(sign * step))
    arrived(zed_s.at[0:NZ - 1], 9)
    fin_s[q] = jnp.sum(zed_s[...], axis=0)

    def spread(step, carry):
        send(fin_s.at[q], fin_s.at[q], 10, q_peer(lax.rem(q + step, NQ)))
        return carry

    lax.fori_loop(1, NQ, spread, 0)
    arrived(fin_s.at[0:NQ - 1], 10)

    def normal(g):
        return g * lax.rsqrt(jnp.mean(g * g) + EPS)

    up_mix_ref[...] = normal(fin_s[0:16, 0:8, :].reshape(C, C))
    up_out_ref[...] = normal(fin_s[16:32, 0:8, :].reshape(C, C))
    up_stem_ref[...] = normal(jnp.concatenate([fin_s[tile, 8:12, :] for tile in range(16)], axis=0))
    up_proj_ref[...] = normal(jnp.concatenate([fin_s[16 + tile, 8:12, :] for tile in range(16)], axis=0)).T

    sent(emb_s.at[0, 0:2 * NEAR], 0)
    sent(cnt_s.at[0, 0:2 * NEAR], 1)
    sent(emb_s.at[0, 0:far], 2)
    sent(cnt_s.at[0, 0:far], 3)
    sent(emb_s.at[0:NP - 1, 0:2 * NEAR + 1], 4)
    sent(emb_s.at[0:NP - 1, 0:far], 5)
    sent(cnt_s.at[0:NP - 1], 6)
    sent(tot_s.at[0:NP - 1], 7)
    sent(gath_s.at[0:NQ - 1], 8)
    sent(zed_s.at[0:NZ - 1], 9)
    sent(fin_s.at[0:NQ - 1], 10)


def on_device(cutouts, counts, partner, w_stem, w_mix, w_out, w_proj):
    vmem = pl.BlockSpec(memory_space=pltpu.VMEM)
    outs = pl.pallas_call(
        kernel,
        out_shape=(
            jax.ShapeDtypeStruct((VOX, C), F32),
            jax.ShapeDtypeStruct((C, C), F32),
            jax.ShapeDtypeStruct((C, C), F32),
            jax.ShapeDtypeStruct((C, E), F32),
            jax.ShapeDtypeStruct((1, HALF), F32),
        ),
        in_specs=[vmem, pl.BlockSpec(memory_space=pltpu.SMEM)] + [vmem] * 5,
        out_specs=(vmem,) * 5,
        scratch_shapes=[
            pltpu.VMEM((ROWS, 128), BF16),
            pltpu.VMEM((ROWS, 2 * C), BF16),
            pltpu.VMEM((ROWS, 2 * C), F32),
            pltpu.VMEM((ROWS, 2 * C), F32),
            pltpu.VMEM((128, ROWS), BF16),
            pltpu.VMEM((2 * C, ROWS), BF16),
            pltpu.VMEM((NP, NZ, HALF, 128), BF16),
            pltpu.VMEM((NP, NZ, 1, 128), F32),
            pltpu.VMEM((NP, 2, LINE), F32),
            pltpu.VMEM((NQ, 12, 128), F32),
            pltpu.VMEM((NQ, 12, 128), F32),
            pltpu.VMEM((NZ, 12, 128), F32),
            pltpu.VMEM((NQ, 12, 128), F32),
            pltpu.SemaphoreType.DMA((11,)),
            pltpu.SemaphoreType.DMA((11,)),
        ],
        compiler_params=pltpu.CompilerParams(
            collective_id=0, has_side_effects=True, vmem_limit_bytes=40 * 1024 * 1024
        ),
    )(cutouts[0], counts, partner, w_stem, w_mix, w_out, w_proj)
    return outs[:4] + (outs[4][None],)


def solution(mesh):
    in_specs = (P("rep", "vol", None), P("rep", "vol"), P("rep", None), P(), P(), P(), P())
    out_specs = (P(), P(), P(), P(), P("rep", "vol", None))
    return jax.shard_map(
        on_device, mesh=mesh, in_specs=in_specs, out_specs=out_specs, check_vma=False
    )
```

time: 1530 us -> 62.5 us (0.04)
  waiting for transfers between devices: 930 us -> 0 us
  blocking collectives: 366 us -> 0 us
  starting transfers between devices: 171 us -> 0 us
  Pallas kernels: 0 us -> 54.5 us
  other arithmetic: 17.8 us -> 0 us
  between operations: 18.5 us -> 1.34 us
    psum x2 -> x0, waiting for transfers between devices: 873 us -> none  [on_device(): lax.psum((grads[0], grads[1], grads[2], grads[3]), ('vol', 'rep'))]
    unnamed x2 -> x0, blocking collectives: 281 us -> none
    all_to_all x2 -> x0, starting transfers between devices: 171 us -> none  [the longest x1 165 us: on_device(): lax.all_to_all(send_ids, 'vol', split_axis=0, concat_axis=0, tiled=True)]
    all_gather x1 -> x0, blocking collectives: 85.6 us -> none  [on_device(): lax.all_gather(anchor_feature_matrix, 'vol', axis=0, tiled=True)]
    all_to_all x2 -> x0, waiting for transfers between devices: 57.5 us -> none  [the longest x1 47.7 us: on_device(): lax.all_to_all(packed, 'vol', split_axis=0, concat_axis=0, tiled=True)]
    pallas_call x0 -> x1, Pallas kernels: none -> 54.5 us  [on_device(): pl.pallas_call(kernel, out_shape=(jax.ShapeDtypeStruct((VOX, C), F32), ja...]
  transfers between devices with their start and end apart: 4 -> 0, of which waited for: 4 -> 0; matrix products, arithmetic and copies ran while one was open for 1% -> 0% of each run, Pallas kernels for 0% -> 0%
where the time goes in v1:
time: 62.5 us; the launch traced here: 62.2 us
  Pallas kernels  54.5 us (87%)
  local copies, waits for them, and re-layouts  6.32 us (10%)
  between operations  1.34 us (2%)
    pallas_call x1, Pallas kernels, on_device(): pl.pallas_call(kernel, out_shape=(jax.ShapeDtypeStruct((VOX, C), F32), ja...  54.5 us
    unnamed x16, local copies, waits for them, and re-layouts  6.32 us

profile of v1, /device:TPU:1, one launch (start us, length us, event | category | flops | bytes accessed | tf_op | source)
XLA Modules:
  0.0 62.2 jit_solution(3914113310377973831)
XLA Ops:
  0.6 0.0 copy-start.1
  1.3 0.0 copy-start.3
  1.3 0.8 %copy.12.proj_ref = bf16[128,64]{1,0:T(8,128)(2,1)S(1)} copy(bf16[128,64]{0,1:T(8,128)(2,1)} %param.13) | data formatting | bytes 32768 | tf_op args[6]
  2.1 0.0 copy-done.1
  2.1 0.0 copy-done.3
  2.2 0.0 copy-start
  2.2 0.9 %copy-done = bf16[1,32,4096]{2,1,0:T(8,128)(2,1)S(1)} copy-done((bf16[1,32,4096]{2,1,0:T(8,128)(2,1)S(1)}, bf16[1,32,4096]{2,1,0:T(8,128)(2,1)}, u32[]{:S(2)}) %copy-start) | copy-done | bytes 262168
  3.1 0.0 copy-start.2
  3.1 0.8 %copy-done.2 = bf16[128,128]{1,0:T(8,128)(2,1)S(1)} copy-done((bf16[128,128]{1,0:T(8,128)(2,1)S(1)}, bf16[128,128]{1,0:T(8,128)(2,1)}, u32[]{:S(2)}) %copy-start.2) | copy-done | bytes 32792
  3.9 0.0 copy-start.4
  3.9 0.7 %copy-done.4 = s32[1,2048]{1,0:T(1,128)S(1)} copy-done((s32[1,2048]{1,0:T(1,128)S(1)}, s32[1,2048]{1,0:T(1,128)}, u32[]{:S(2)}) %copy-start.4) | copy-done | bytes 8216
  4.6 54.5 %shard_map.110 = (f32[64,128]{1,0:T(8,128)S(1)}, f32[128,128]{1,0:T(8,128)S(1)}, f32[128,128]{1,0:T(8,128)S(1)}, f32[128,64]{1,0:T(8,128)S(1)}, f32[1,16]{1,0:T(1,128)S(1)}) custom-call(bf16[32,4096]{1,0:T(8,128)(2,1)S(1)} %bitcast.2, s32[1,1]{1,0:T(1,128)S(6)} %copy.18.count_ref, s32[1,2048]{1,0:T(1,128)S(1)} %copy-done.4, bf16[64,128]{1,0:T(8,128)(2,1)S(1)} %copy-done.3, ...), custom_call_target="tpu_custom_call" | custom-call | tf_op jit(solution)/shard_map/pallas_call | solution.py:380
  59.1 0.7 %copy.13 = f32[128,64]{0,1:T(8,128)} copy(f32[128,64]{1,0:T(8,128)S(1)} %get-tuple-element.18) | data formatting | bytes 65536
  59.8 0.6 copy.19
  60.4 0.6 %copy.20 = f32[128,128]{1,0:T(8,128)} copy(f32[128,128]{1,0:T(8,128)S(1)} %get-tuple-element.26) | data formatting | bytes 131072
  61.0 0.6 %copy.21 = f32[128,128]{1,0:T(8,128)} copy(f32[128,128]{1,0:T(8,128)S(1)} %get-tuple-element.27) | data formatting | bytes 131072
  61.7 0.5 copy.22
Async XLA Ops:
  0.6 1.5 %copy-start.1 = (bf16[128,128]{1,0:T(8,128)(2,1)S(1)}, bf16[128,128]{1,0:T(8,128)(2,1)}, u32[]{:S(2)}) copy-start(bf16[128,128]{1,0:T(8,128)(2,1)} %mix_ref.1) | copy-start | bytes 98308
  1.3 0.9 %copy-start.3 = (bf16[64,128]{1,0:T(8,128)(2,1)S(1)}, bf16[64,128]{1,0:T(8,128)(2,1)}, u32[]{:S(2)}) copy-start(bf16[64,128]{1,0:T(8,128)(2,1)} %stem_ref.1) | copy-start | bytes 49156
  2.2 1.0 %copy-start = (bf16[1,32,4096]{2,1,0:T(8,128)(2,1)S(1)}, bf16[1,32,4096]{2,1,0:T(8,128)(2,1)}, u32[]{:S(2)}) copy-start(bf16[1,32,4096]{2,1,0:T(8,128)(2,1)} %param.7) | copy-start | bytes 786436
  3.1 0.8 %copy-start.2 = (bf16[128,128]{1,0:T(8,128)(2,1)S(1)}, bf16[128,128]{1,0:T(8,128)(2,1)}, u32[]{:S(2)}) copy-start(bf16[128,128]{1,0:T(8,128)(2,1)} %out_ref.1) | copy-start | bytes 98308
  3.9 0.7 %copy-start.4 = (s32[1,2048]{1,0:T(1,128)S(1)}, s32[1,2048]{1,0:T(1,128)}, u32[]{:S(2)}) copy-start(s32[1,2048]{1,0:T(1,128)} %partner_ref.1) | copy-start | bytes 24580

commit v2 on v1

--- a/solution.py
+++ b/solution.py
@@ -67,8 +67,9 @@
 
 
 def kernel(
-    cut_ref, count_ref, partner_ref, stem_ref, mix_ref, out_ref, proj_ref,
-    up_stem_ref, up_mix_ref, up_out_ref, up_proj_ref, loss_ref,
+    cut_hbm, count_hbm, partner_hbm, stem_hbm, mix_hbm, out_hbm, proj_hbm,
+    up_ref, loss_ref,
+    cut_ref, count_ref, partner_ref, stem_ref, mix_ref, out_ref, proj_ref, load_sem,
     x_s, hid_s, slope1_s, slope2_s, xt_s, ht_s,
     emb_s, cnt_s, tot_s, part_s, gath_s, zed_s, fin_s,
     send_sem, recv_sem,
@@ -99,6 +100,16 @@
 
     def sent(ref, kind):
         pltpu.make_async_copy(ref, ref, send_sem.at[kind]).wait()
+
+    loads = [
+        pltpu.make_async_copy(source, target, load_sem.at[number])
+        for number, (source, target) in enumerate([
+            (cut_hbm, cut_ref), (stem_hbm, stem_ref), (mix_hbm, mix_ref), (count_hbm, count_ref),
+            (out_hbm, out_ref), (proj_hbm, proj_ref), (partner_hbm, partner_ref),
+        ])
+    ]
+    for load in loads:
+        load.start()
 
     barrier = pltpu.get_barrier_semaphore()
     greeted = 0
@@ -115,8 +126,10 @@
         pl.semaphore_signal(barrier, inc=1, device_id=p_peer(step), device_id_type=MESH)
         greeted += 1
 
-    count = count_ref[0, 0]
-    cnt_s[p, NEAR] = jnp.full((1, 128), count, jnp.int32).astype(F32)
+    for load in loads:
+        load.wait()
+    count = count_ref[...]
+    cnt_s[p, NEAR] = jnp.broadcast_to(count, (1, 128)).astype(F32)
     w_stem2 = block_diagonal(stem_ref[...])
     w_mix2 = block_diagonal(mix_ref[...])
     for pair in range(PAIRS):
@@ -143,7 +156,7 @@
     hid_sum, mix_sum = fold(hid_sum), fold(mix_sum)
     w_out = out_ref[...]
     pooled = ((hid_sum + dot(mix_sum, w_out.astype(F32), HIGHEST)) * (1.0 / PATCHES)).astype(BF16)
-    raw = dot(pooled, proj_ref[...])
+    raw = dot_nt(pooled, proj_ref[...])
     inv_norm = lax.rsqrt(jnp.sum(raw * raw, axis=1, keepdims=True) + EPS)
     unit = raw * inv_norm
     live = iota((SLOTS, E), 0) < count
@@ -201,24 +214,24 @@
         axis=0,
     )
 
-    def scores(part):
-        block = emb_s[part].reshape(LINE, 128)
-        return jnp.exp2(dot_nt(block, columns) * SCALE)
-
     def add_rows(e):
-        return jnp.sum(e.reshape(LINE // 8, 8, 4 * LINE), axis=0)
+        return jnp.sum(e.reshape(e.shape[0] // 8, 8, 4 * LINE), axis=0)
 
     col = iota((LINE, 4 * LINE), 1)
     row = iota((LINE, 4 * LINE), 0)
     self_score = (col == row) | (col == row + 3 * LINE)
-    total = add_rows(jnp.where(self_score, 0.0, scores(p)))
+    total = add_rows(jnp.where(self_score, 0.0, jnp.exp2(dot_nt(line, columns) * SCALE)))
+
+    def other(first, last):
+        def add(step, total):
+            block = emb_s[lax.rem(p + step, NP), first:last].reshape((last - first) * HALF, 128)
+            return total + add_rows(jnp.exp2(dot_nt(block, columns) * SCALE))
+        return add
+
     arrived(emb_s.at[0:NP - 1, 0:2 * NEAR + 1], 4)
+    total = lax.fori_loop(1, NP, other(0, 2 * NEAR + 1), total)
     arrived(emb_s.at[0:NP - 1, 0:far], 5)
-
-    def other(step, total):
-        return total + add_rows(scores(lax.rem(p + step, NP)))
-
-    total = lax.fori_loop(1, NP, other, total)
+    total = lax.fori_loop(1, NP, other(2 * NEAR + 1, NZ), total)
     line_sum = fold(jnp.sum(total, axis=0, keepdims=True)) - float(DEAD)
     tot_s[p] = jnp.concatenate([line_sum[:, :LINE], line_sum[:, LINE:]], axis=0)
     own_total = tot_s.at[p]
@@ -295,15 +308,32 @@
     radial = jnp.sum(unit * d_embed, axis=1, keepdims=True)
     d_raw = jnp.where(live, inv_norm * (d_embed - unit * radial), 0.0).astype(BF16)
     g_proj = dot_tn(d_raw, pooled)
-    d_sum = (dot_nt(d_raw, proj_ref[...]) * (1.0 / PATCHES)).astype(BF16)
+    d_sum = (dot(d_raw, proj_ref[...]) * (1.0 / PATCHES)).astype(BF16)
     d_sum32 = d_sum.astype(F32)
     g_out = dot_tn(mix_sum, d_sum32, HIGHEST)
     d_mixed = twice(dot_nt(d_sum, w_out))
     d_spread = twice(d_sum32)
 
-    for tile in range(NP * 2):
+    def scatter(first):
+        def one(step, carry):
+            to = first + lax.rem(q + step, NQ // 2)
+            send(part_s.at[to], gath_s.at[q], 8, q_peer(to))
+            return carry
+
+        inside = (q // (NQ // 2) == first // (NQ // 2))
+
+        @pl.when(inside)
+        def _():
+            lax.fori_loop(1, NQ // 2, one, 0)
+
+        @pl.when(jnp.logical_not(inside))
+        def _():
+            lax.fori_loop(0, NQ // 2, one, 0)
+
+    for tile in range(NQ // 2):
         part_s[16 + tile, 0:8, :] = g_out[tile * 8:(tile + 1) * 8]
         part_s[16 + tile, 8:12, :] = g_proj[tile * 4:(tile + 1) * 4]
+    scatter(NQ // 2)
 
     g_mix = jnp.zeros((2 * C, 2 * C), F32)
     g_stem = jnp.zeros((2 * VOX, 2 * C), F32)
@@ -317,16 +347,11 @@
         g_stem = g_stem + dot(xt_s[:, rows], d_pre1)
     g_mix = g_mix[:C, :C] + g_mix[C:, C:]
     g_stem = g_stem[:VOX, :C] + g_stem[VOX:, C:]
-    for tile in range(NP * 2):
+    for tile in range(NQ // 2):
         part_s[tile, 0:8, :] = g_mix[tile * 8:(tile + 1) * 8]
         part_s[tile, 8:12, :] = g_stem[tile * 4:(tile + 1) * 4]
 
-    def scatter(step, carry):
-        to = lax.rem(q + step, NQ)
-        send(part_s.at[to], gath_s.at[q], 8, q_peer(to))
-        return carry
-
-    lax.fori_loop(1, NQ, scatter, 0)
+    scatter(0)
     gath_s[q] = part_s[q]
 
     out_sum = jnp.zeros((HALF, 1), F32)
@@ -357,10 +382,10 @@
     def normal(g):
         return g * lax.rsqrt(jnp.mean(g * g) + EPS)
 
-    up_mix_ref[...] = normal(fin_s[0:16, 0:8, :].reshape(C, C))
-    up_out_ref[...] = normal(fin_s[16:32, 0:8, :].reshape(C, C))
-    up_stem_ref[...] = normal(jnp.concatenate([fin_s[tile, 8:12, :] for tile in range(16)], axis=0))
-    up_proj_ref[...] = normal(jnp.concatenate([fin_s[16 + tile, 8:12, :] for tile in range(16)], axis=0)).T
+    up_ref[0:64] = normal(jnp.concatenate([fin_s[tile, 8:12, :] for tile in range(16)], axis=0))
+    up_ref[64:192] = normal(fin_s[0:16, 0:8, :].reshape(C, C))
+    up_ref[192:320] = normal(fin_s[16:32, 0:8, :].reshape(C, C))
+    up_ref[320:384] = normal(jnp.concatenate([fin_s[16 + tile, 8:12, :] for tile in range(16)], axis=0))
 
     sent(emb_s.at[0, 0:2 * NEAR], 0)
     sent(cnt_s.at[0, 0:2 * NEAR], 1)
@@ -375,20 +400,31 @@
     sent(fin_s.at[0:NQ - 1], 10)
 
 
+def store(up_ref, loss_ref, stem_ref, mix_ref, out_ref, proj_ref, out_loss_ref):
+    stem_ref[...] = up_ref[0:64]
+    mix_ref[...] = up_ref[64:192]
+    out_ref[...] = up_ref[192:320]
+    proj_ref[...] = up_ref[320:384]
+    out_loss_ref[...] = loss_ref[...]
+
+
 def on_device(cutouts, counts, partner, w_stem, w_mix, w_out, w_proj):
     vmem = pl.BlockSpec(memory_space=pltpu.VMEM)
-    outs = pl.pallas_call(
+    hbm = pl.BlockSpec(memory_space=pltpu.HBM)
+    updates, loss = pl.pallas_call(
         kernel,
-        out_shape=(
-            jax.ShapeDtypeStruct((VOX, C), F32),
-            jax.ShapeDtypeStruct((C, C), F32),
-            jax.ShapeDtypeStruct((C, C), F32),
-            jax.ShapeDtypeStruct((C, E), F32),
-            jax.ShapeDtypeStruct((1, HALF), F32),
-        ),
-        in_specs=[vmem, pl.BlockSpec(memory_space=pltpu.SMEM)] + [vmem] * 5,
-        out_specs=(vmem,) * 5,
+        out_shape=(jax.ShapeDtypeStruct((384, 128), F32), jax.ShapeDtypeStruct((1, HALF), F32)),
+        in_specs=[hbm] * 7,
+        out_specs=(vmem,) * 2,
         scratch_shapes=[
+            pltpu.VMEM((SLOTS, PATCHES * VOX), BF16),
+            pltpu.VMEM((1, 1), jnp.int32),
+            pltpu.VMEM((1, NODES), jnp.int32),
+            pltpu.VMEM((VOX, C), BF16),
+            pltpu.VMEM((C, C), BF16),
+            pltpu.VMEM((C, C), BF16),
+            pltpu.VMEM((E, C), BF16),
+            pltpu.SemaphoreType.DMA((7,)),
             pltpu.VMEM((ROWS, 128), BF16),
             pltpu.VMEM((ROWS, 2 * C), BF16),
             pltpu.VMEM((ROWS, 2 * C), F32),
@@ -406,10 +442,22 @@
             pltpu.SemaphoreType.DMA((11,)),
         ],
         compiler_params=pltpu.CompilerParams(
-            collective_id=0, has_side_effects=True, vmem_limit_bytes=40 * 1024 * 1024
+            collective_id=0, has_side_effects=True, vmem_limit_bytes=56 * 1024 * 1024
         ),
-    )(cutouts[0], counts, partner, w_stem, w_mix, w_out, w_proj)
-    return outs[:4] + (outs[4][None],)
+    )(cutouts[0], counts, partner, w_stem, w_mix, w_out, w_proj.T)
+    outs = pl.pallas_call(
+        store,
+        out_shape=(
+            jax.ShapeDtypeStruct((VOX, C), F32),
+            jax.ShapeDtypeStruct((C, C), F32),
+            jax.ShapeDtypeStruct((C, C), F32),
+            jax.ShapeDtypeStruct((E, C), F32),
+            jax.ShapeDtypeStruct((1, HALF), F32),
+        ),
+        in_specs=[vmem] * 2,
+        out_specs=(vmem,) * 5,
+    )(updates, loss)
+    return outs[:3] + (outs[3].T, outs[4][None])
 
 
 def solution(mesh):

time: 62.5 us -> 58.2 us (0.931)
  local copies, waits for them, and re-layouts: 6.32 us -> 0 us
  Pallas kernels: 54.5 us -> 56.7 us
    unnamed x16 -> x0, local copies, waits for them, and re-layouts: 6.32 us -> none
    pallas_call x1 -> x2, Pallas kernels: 54.5 us -> 56.7 us  [the longest x1 55.1 us: on_device(): pl.pallas_call(kernel, out_shape=(jax.ShapeDtypeStruct((384, 128), F32),...]
where the time goes in v2:
time: 58.2 us; the launch traced here: 58 us
  Pallas kernels  56.7 us (97%)
  between operations  1.29 us (2%)
    pallas_call x1, Pallas kernels, on_device(): pl.pallas_call(kernel, out_shape=(jax.ShapeDtypeStruct((384, 128), F32),...  55.1 us
    pallas_call x1, Pallas kernels, on_device(): pl.pallas_call(store, out_shape=(jax.ShapeDtypeStruct((VOX, C), F32), jax...  1.61 us

profile of v2, /device:TPU:1, one launch (start us, length us, event | category | flops | bytes accessed | tf_op | source)
XLA Modules:
  0.0 58.0 jit_solution(14687664054798444737)
XLA Ops:
  1.3 55.1 %shard_map.110 = (f32[384,128]{1,0:T(8,128)}, f32[1,16]{1,0:T(1,128)}) custom-call(bf16[32,4096]{1,0:T(8,128)(2,1)} %bitcast.4, s32[1,1]{1,0:T(1,128)S(6)} %copy.12.count_hbm, s32[1,2048]{1,0:T(1,128)} %partner_hbm.1, bf16[64,128]{1,0:T(8,128)(2,1)} %stem_hbm.1, bf16[128,128]{1,0:T(8,128)(2,1)} %mix_hbm.1, bf16[128,128]{1,0:T(8,128)(2,1)} %out_hbm.1, ...), custom_call_target="tpu_custom_call" | custom-call | tf_op jit(solution)/shard_map/pallas_call | solution.py:414
  56.4 1.6 %shard_map.111 = (f32[64,128]{1,0:T(8,128)}, f32[128,128]{1,0:T(8,128)}, f32[128,128]{1,0:T(8,128)}, f32[64,128]{1,0:T(8,128)}, f32[1,16]{1,0:T(1,128)}) custom-call(f32[384,128]{1,0:T(8,128)} %get-tuple-element.12.up_ref, f32[1,16]{1,0:T(1,128)} %get-tuple-element.13.loss_ref), custom_call_target="tpu_custom_call" | custom-call | tf_op jit(solution)/shard_map/pallas_call | solution.py:448

commit v3 on v2

--- a/solution.py
+++ b/solution.py
@@ -28,6 +28,9 @@
 LOG2E = 1.4426950408889634
 SCALE = LOG2E / TEMPERATURE
 EPS = 1e-6
+(LINE_NEAR_A, LINE_NEAR_B, LINE_FAR_A, LINE_FAR_B, PLANE_NEAR_A, PLANE_NEAR_B, PLANE_FAR_A, PLANE_FAR_B,
+ COUNT_NEAR, COUNT_FAR, PLANE_COUNT, TOTAL, PIECE, PIECE_Z, RESULT) = range(15)
+KINDS = 15
 
 
 def iota(shape, dim):
@@ -42,8 +45,8 @@
     return lax.dot_general(a, b, (((1,), (1,)), ((), ())), preferred_element_type=F32)
 
 
-def dot_tn(a, b, precision=None):
-    return lax.dot_general(a, b, (((0,), (0,)), ((), ())), precision=precision, preferred_element_type=F32)
+def dot_tn(a, b):
+    return lax.dot_general(a, b, (((0,), (0,)), ((), ())), preferred_element_type=F32)
 
 
 def sigmoid(v):
@@ -169,38 +172,52 @@
     own_count = cnt_s.at[p, NEAR]
     for step in range(NEAR, 0, -1):
         for sign in (1, -1):
-            send(own, emb_s.at[p, NEAR - sign * step], 0, z_peer(sign * step))
+            send(own, emb_s.at[p, NEAR - sign * step], LINE_NEAR_B if step > 2 else LINE_NEAR_A, z_peer(sign * step))
     for step in range(NEAR, 0, -1):
         for sign in (1, -1):
-            send(own_count, cnt_s.at[p, NEAR - sign * step], 1, z_peer(sign * step))
+            send(own_count, cnt_s.at[p, NEAR - sign * step], COUNT_NEAR, z_peer(sign * step))
+
+    def share(first, last, kind):
+        block = emb_s.at[p, first:last]
+        for step in range(1, NP):
+            send(block, block, kind, p_peer(step))
+
+    def relay(source, target, blocks, kind, towards, ref=emb_s):
+        send(ref.at[p, source:source + blocks], ref.at[p, target:target + blocks], kind, z_peer(towards))
 
     xt_s[...] = x_s[...].T
     ht_s[...] = hid_s[...].T
-    lane = iota((HALF, 128), 1)
-    zero_half = jnp.zeros((HALF, E), BF16)
+    terms, rest = [], mix_sum
+    for _ in range(3):
+        terms.append(rest.astype(BF16))
+        rest = rest - terms[-1].astype(F32)
+    mix_terms = jnp.concatenate(terms, axis=0).T
     zero_slots = jnp.zeros((SLOTS, E), BF16)
     anchors = jnp.concatenate(
         [jnp.concatenate([embed, zero_slots], axis=1), jnp.concatenate([zero_slots, embed], axis=1)], axis=0
     )
 
-    arrived(emb_s.at[0, 0:2 * NEAR], 0)
-    far = NZ - 2 * NEAR - 1
-    send(emb_s.at[p, NEAR + 1:2 * NEAR + 1], emb_s.at[p, 2 * NEAR + 1:3 * NEAR + 1], 2, z_peer(-NEAR))
-    send(emb_s.at[p, 1:NEAR], emb_s.at[p, 3 * NEAR + 1:4 * NEAR], 2, z_peer(NEAR))
-    arrived(cnt_s.at[0, 0:2 * NEAR], 1)
-    send(cnt_s.at[p, NEAR + 1:2 * NEAR + 1], cnt_s.at[p, 2 * NEAR + 1:3 * NEAR + 1], 3, z_peer(-NEAR))
-    send(cnt_s.at[p, 1:NEAR], cnt_s.at[p, 3 * NEAR + 1:4 * NEAR], 3, z_peer(NEAR))
-    near_block = emb_s.at[p, 0:2 * NEAR + 1]
-    for step in range(1, NP):
-        send(near_block, near_block, 4, p_peer(step))
-    arrived(emb_s.at[0, 0:far], 2)
-    far_block = emb_s.at[p, 2 * NEAR + 1:NZ]
-    for step in range(1, NP):
-        send(far_block, far_block, 5, p_peer(step))
-    arrived(cnt_s.at[0, 0:far], 3)
+    arrived(emb_s.at[0, 0:4], LINE_NEAR_A)
+    relay(5, 9, 2, LINE_FAR_A, -NEAR)
+    relay(2, 14, 2, LINE_FAR_A, NEAR)
+    share(2, 7, PLANE_NEAR_A)
+    arrived(emb_s.at[0, 0:4], LINE_NEAR_B)
+    relay(7, 11, 2, LINE_FAR_B, -NEAR)
+    relay(1, 13, 1, LINE_FAR_B, NEAR)
+    share(0, 2, PLANE_NEAR_B)
+    share(7, 9, PLANE_NEAR_B)
+    arrived(cnt_s.at[0, 0:8], COUNT_NEAR)
+    relay(5, 9, 4, COUNT_FAR, -NEAR, cnt_s)
+    relay(1, 13, 3, COUNT_FAR, NEAR, cnt_s)
+    arrived(emb_s.at[0, 0:4], LINE_FAR_A)
+    share(9, 11, PLANE_FAR_A)
+    share(14, 16, PLANE_FAR_A)
+    arrived(emb_s.at[0, 0:3], LINE_FAR_B)
+    share(11, 14, PLANE_FAR_B)
+    arrived(cnt_s.at[0, 0:7], COUNT_FAR)
     count_block = cnt_s.at[p]
     for step in range(1, NP):
-        send(count_block, count_block, 6, p_peer(step))
+        send(count_block, count_block, PLANE_COUNT, p_peer(step))
 
     line = emb_s[p].reshape(LINE, 128)
     low = iota((LINE, 128), 1) < E
@@ -214,29 +231,36 @@
         axis=0,
     )
 
-    def add_rows(e):
-        return jnp.sum(e.reshape(e.shape[0] // 8, 8, 4 * LINE), axis=0)
-
-    col = iota((LINE, 4 * LINE), 1)
-    row = iota((LINE, 4 * LINE), 0)
-    self_score = (col == row) | (col == row + 3 * LINE)
-    total = add_rows(jnp.where(self_score, 0.0, jnp.exp2(dot_nt(line, columns) * SCALE)))
-
-    def other(first, last):
-        def add(step, total):
-            block = emb_s[lax.rem(p + step, NP), first:last].reshape((last - first) * HALF, 128)
-            return total + add_rows(jnp.exp2(dot_nt(block, columns) * SCALE))
-        return add
-
-    arrived(emb_s.at[0:NP - 1, 0:2 * NEAR + 1], 4)
-    total = lax.fori_loop(1, NP, other(0, 2 * NEAR + 1), total)
-    arrived(emb_s.at[0:NP - 1, 0:far], 5)
-    total = lax.fori_loop(1, NP, other(2 * NEAR + 1, NZ), total)
-    line_sum = fold(jnp.sum(total, axis=0, keepdims=True)) - float(DEAD)
+    def powers(block, against):
+        return jnp.exp2(dot_nt(block, against) * SCALE)
+
+    def add_rows(total, first, last):
+        block = emb_s[:, first:last].reshape(NP * (last - first) * HALF, 128)
+        e = powers(block, columns)
+        return total + jnp.sum(e.reshape(e.shape[0] // 8, 8, 4 * LINE), axis=0)
+
+    diagonal = iota((LINE, LINE), 0) == iota((LINE, LINE), 1)
+    self_sum = jnp.concatenate(
+        [
+            jnp.sum(jnp.where(diagonal, powers(line, columns[at:at + LINE]), 0.0), axis=0, keepdims=True)
+            for at in (0, 3 * LINE)
+        ],
+        axis=1,
+    )
+    total = jnp.zeros((8, 4 * LINE), F32)
+    arrived(emb_s.at[0:NP - 1, 0:5], PLANE_NEAR_A)
+    total = add_rows(total, 2, 7)
+    arrived(emb_s.at[0:NP - 1, 0:4], PLANE_NEAR_B)
+    total = add_rows(add_rows(total, 0, 2), 7, 9)
+    arrived(emb_s.at[0:NP - 1, 0:4], PLANE_FAR_A)
+    total = add_rows(add_rows(total, 9, 11), 14, 16)
+    arrived(emb_s.at[0:NP - 1, 0:3], PLANE_FAR_B)
+    total = add_rows(total, 11, 14)
+    line_sum = fold(jnp.sum(total, axis=0, keepdims=True)) - float(DEAD) - self_sum
     tot_s[p] = jnp.concatenate([line_sum[:, :LINE], line_sum[:, LINE:]], axis=0)
     own_total = tot_s.at[p]
     for step in range(1, NP):
-        send(own_total, own_total, 7, p_peer(step))
+        send(own_total, own_total, TOTAL, p_peer(step))
 
     every = emb_s[...].reshape(NP * LINE, 128)
     wide = NP * LINE
@@ -251,7 +275,7 @@
     own_inv = 1.0 / own_sum
     row_weight = (exps * jnp.concatenate([own_inv, own_inv], axis=0)).astype(BF16)
 
-    arrived(cnt_s.at[0:NP - 1], 6)
+    arrived(cnt_s.at[0:NP - 1], PLANE_COUNT)
     counts = cnt_s[...]
     by_plane = jnp.sum(counts, axis=0)
 
@@ -294,7 +318,7 @@
     chosen = first[2 * SLOTS:2 * SLOTS + n_pick, :E] + first[2 * SLOTS + n_pick:, E:]
     companion = chosen[:SLOTS]
 
-    arrived(tot_s.at[0:NP - 1], 7)
+    arrived(tot_s.at[0:NP - 1], TOTAL)
     sums = [
         jnp.concatenate([tot_s[part, half:half + 1, :] for part in range(NP)], axis=1) for half in range(2)
     ]
@@ -310,14 +334,14 @@
     g_proj = dot_tn(d_raw, pooled)
     d_sum = (dot(d_raw, proj_ref[...]) * (1.0 / PATCHES)).astype(BF16)
     d_sum32 = d_sum.astype(F32)
-    g_out = dot_tn(mix_sum, d_sum32, HIGHEST)
+    g_out = dot(mix_terms, jnp.concatenate([d_sum] * 3, axis=0))
     d_mixed = twice(dot_nt(d_sum, w_out))
     d_spread = twice(d_sum32)
 
     def scatter(first):
         def one(step, carry):
             to = first + lax.rem(q + step, NQ // 2)
-            send(part_s.at[to], gath_s.at[q], 8, q_peer(to))
+            send(part_s.at[to], gath_s.at[q], PIECE, q_peer(to))
             return carry
 
         inside = (q // (NQ // 2) == first // (NQ // 2))
@@ -363,21 +387,21 @@
     square = iota((HALF, HALF), 0) == iota((HALF, HALF), 1)
     loss_ref[...] = jnp.sum(jnp.where(square, loss, 0.0), axis=0, keepdims=True)
 
-    arrived(gath_s.at[0:NQ - 1], 8)
+    arrived(gath_s.at[0:NQ - 1], PIECE)
     zed_s[z] = jnp.sum(gath_s[...], axis=0)
     for step in range(NZ // 2, 0, -1):
         for sign in (1, -1):
             if step < NZ // 2 or sign == 1:
-                send(zed_s.at[z], zed_s.at[z], 9, z_peer(sign * step))
-    arrived(zed_s.at[0:NZ - 1], 9)
+                send(zed_s.at[z], zed_s.at[z], PIECE_Z, z_peer(sign * step))
+    arrived(zed_s.at[0:NZ - 1], PIECE_Z)
     fin_s[q] = jnp.sum(zed_s[...], axis=0)
 
     def spread(step, carry):
-        send(fin_s.at[q], fin_s.at[q], 10, q_peer(lax.rem(q + step, NQ)))
+        send(fin_s.at[q], fin_s.at[q], RESULT, q_peer(lax.rem(q + step, NQ)))
         return carry
 
     lax.fori_loop(1, NQ, spread, 0)
-    arrived(fin_s.at[0:NQ - 1], 10)
+    arrived(fin_s.at[0:NQ - 1], RESULT)
 
     def normal(g):
         return g * lax.rsqrt(jnp.mean(g * g) + EPS)
@@ -387,17 +411,15 @@
     up_ref[192:320] = normal(fin_s[16:32, 0:8, :].reshape(C, C))
     up_ref[320:384] = normal(jnp.concatenate([fin_s[16 + tile, 8:12, :] for tile in range(16)], axis=0))
 
-    sent(emb_s.at[0, 0:2 * NEAR], 0)
-    sent(cnt_s.at[0, 0:2 * NEAR], 1)
-    sent(emb_s.at[0, 0:far], 2)
-    sent(cnt_s.at[0, 0:far], 3)
-    sent(emb_s.at[0:NP - 1, 0:2 * NEAR + 1], 4)
-    sent(emb_s.at[0:NP - 1, 0:far], 5)
-    sent(cnt_s.at[0:NP - 1], 6)
-    sent(tot_s.at[0:NP - 1], 7)
-    sent(gath_s.at[0:NQ - 1], 8)
-    sent(zed_s.at[0:NZ - 1], 9)
-    sent(fin_s.at[0:NQ - 1], 10)
+    for kind, ref in [
+        (LINE_NEAR_A, emb_s.at[0, 0:4]), (LINE_NEAR_B, emb_s.at[0, 0:4]), (COUNT_NEAR, cnt_s.at[0, 0:8]),
+        (LINE_FAR_A, emb_s.at[0, 0:4]), (LINE_FAR_B, emb_s.at[0, 0:3]), (COUNT_FAR, cnt_s.at[0, 0:7]),
+        (PLANE_NEAR_A, emb_s.at[0:NP - 1, 0:5]), (PLANE_NEAR_B, emb_s.at[0:NP - 1, 0:4]),
+        (PLANE_FAR_A, emb_s.at[0:NP - 1, 0:4]), (PLANE_FAR_B, emb_s.at[0:NP - 1, 0:3]),
+        (PLANE_COUNT, cnt_s.at[0:NP - 1]), (TOTAL, tot_s.at[0:NP - 1]), (PIECE, gath_s.at[0:NQ - 1]),
+        (PIECE_Z, zed_s.at[0:NZ - 1]), (RESULT, fin_s.at[0:NQ - 1]),
+    ]:
+        sent(ref, kind)
 
 
 def store(up_ref, loss_ref, stem_ref, mix_ref, out_ref, proj_ref, out_loss_ref):
@@ -438,8 +460,8 @@
             pltpu.VMEM((NQ, 12, 128), F32),
             pltpu.VMEM((NZ, 12, 128), F32),
             pltpu.VMEM((NQ, 12, 128), F32),
-            pltpu.SemaphoreType.DMA((11,)),
-            pltpu.SemaphoreType.DMA((11,)),
+            pltpu.SemaphoreType.DMA((KINDS,)),
+            pltpu.SemaphoreType.DMA((KINDS,)),
         ],
         compiler_params=pltpu.CompilerParams(
             collective_id=0, has_side_effects=True, vmem_limit_bytes=56 * 1024 * 1024

time: 58.2 us -> 55.7 us (0.957)
  Pallas kernels: 56.7 us -> 54.3 us
    pallas_call x1, Pallas kernels: 55.1 us -> 52.7 us  [on_device(): pl.pallas_call(kernel, out_shape=(jax.ShapeDtypeStruct((384, 128), F32),...]
where the time goes in v3:
time: 55.7 us; the launch traced here: 55.6 us
  Pallas kernels  54.3 us (97%)
  between operations  1.29 us (2%)
    pallas_call x1, Pallas kernels, on_device(): pl.pallas_call(kernel, out_shape=(jax.ShapeDtypeStruct((384, 128), F32),...  52.7 us
    pallas_call x1, Pallas kernels, on_device(): pl.pallas_call(store, out_shape=(jax.ShapeDtypeStruct((VOX, C), F32), jax...  1.61 us

profile of v3, /device:TPU:1, one launch (start us, length us, event | category | flops | bytes accessed | tf_op | source)
XLA Modules:
  0.0 55.6 jit_solution(2561312649469786010)
XLA Ops:
  1.3 52.7 %shard_map.110 = (f32[384,128]{1,0:T(8,128)}, f32[1,16]{1,0:T(1,128)}) custom-call(bf16[32,4096]{1,0:T(8,128)(2,1)} %bitcast.4, s32[1,1]{1,0:T(1,128)S(6)} %copy.12.count_hbm, s32[1,2048]{1,0:T(1,128)} %partner_hbm.1, bf16[64,128]{1,0:T(8,128)(2,1)} %stem_hbm.1, bf16[128,128]{1,0:T(8,128)(2,1)} %mix_hbm.1, bf16[128,128]{1,0:T(8,128)(2,1)} %out_hbm.1, ...), custom_call_target="tpu_custom_call" | custom-call | tf_op jit(solution)/shard_map/pallas_call | solution.py:436
  54.0 1.6 %shard_map.111 = (f32[64,128]{1,0:T(8,128)}, f32[128,128]{1,0:T(8,128)}, f32[128,128]{1,0:T(8,128)}, f32[64,128]{1,0:T(8,128)}, f32[1,16]{1,0:T(1,128)}) custom-call(f32[384,128]{1,0:T(8,128)} %get-tuple-element.12.up_ref, f32[1,16]{1,0:T(1,128)} %get-tuple-element.13.loss_ref), custom_call_target="tpu_custom_call" | custom-call | tf_op jit(solution)/shard_map/pallas_call | solution.py:470

commit v4 on v3

--- a/solution.py
+++ b/solution.py
@@ -10,7 +10,6 @@
 MESH = pl.DeviceIdType.MESH
 F32 = jnp.float32
 BF16 = jnp.bfloat16
-HIGHEST = lax.Precision.HIGHEST
 
 NZ, NP, NY = 16, 8, 4
 NV = NZ * NP
@@ -37,8 +36,8 @@
     return lax.broadcasted_iota(jnp.int32, shape, dim)
 
 
-def dot(a, b, precision=None):
-    return lax.dot_general(a, b, (((1,), (0,)), ((), ())), precision=precision, preferred_element_type=F32)
+def dot(a, b):
+    return lax.dot_general(a, b, (((1,), (0,)), ((), ())), preferred_element_type=F32)
 
 
 def dot_nt(a, b):
@@ -50,7 +49,18 @@
 
 
 def sigmoid(v):
-    return 1.0 / (1.0 + jnp.exp(-v))
+    d = 1.0 + jnp.exp(jnp.minimum(-v, 80.0))
+    r = pl.reciprocal(d, approx=True)
+    r = r * (2.0 - d * r)
+    return r * (2.0 - d * r)
+
+
+def exact_terms(v):
+    terms = []
+    for _ in range(3):
+        terms.append(v.astype(BF16))
+        v = v - terms[-1].astype(F32)
+    return jnp.concatenate(terms, axis=0)
 
 
 def twice(v):
@@ -81,16 +91,20 @@
     rep = lax.axis_index("rep")
     z = vol // NP
     p = lax.rem(vol, NP)
-    q = rep * NP + p
+    x, core = p // 2, lax.rem(p, 2)
+    xs = [lax.rem(x + step, 4) for step in range(4)]
+    ys = [lax.rem(rep + step, 4) for step in range(4)]
+    mate = 1 - core
+    piece = core * (NQ // 2) + rep * 4 + x
+    plane = [z * NP + xs[dx] * 2 for dx in range(4)]
+    p_peers = [plane[dx] + to for dx in (2, 1, 3) for to in (core, mate)] + [plane[0] + mate]
+    apart = sorted(
+        [(dy, dx) for dy in range(4) for dx in range(4) if (dy, dx) != (0, 0)],
+        key=lambda step: -min(step[0], 4 - step[0]) - min(step[1], 4 - step[1]),
+    )
 
     def z_peer(step):
         return (lax.rem(z + step + NZ, NZ) * NP + p, rep)
-
-    def p_peer(step):
-        return (z * NP + lax.rem(p + step, NP), rep)
-
-    def q_peer(other):
-        return (z * NP + lax.rem(other, NP), other // NP)
 
     def send(src, dst, kind, device):
         pltpu.make_async_remote_copy(
@@ -107,7 +121,7 @@
     loads = [
         pltpu.make_async_copy(source, target, load_sem.at[number])
         for number, (source, target) in enumerate([
-            (cut_hbm, cut_ref), (stem_hbm, stem_ref), (mix_hbm, mix_ref), (count_hbm, count_ref),
+            (stem_hbm, stem_ref), (cut_hbm, cut_ref), (mix_hbm, mix_ref), (count_hbm, count_ref),
             (out_hbm, out_ref), (proj_hbm, proj_ref), (partner_hbm, partner_ref),
         ])
     ]
@@ -122,43 +136,41 @@
             greeted += 1
     for step in range(1, NY):
         pl.semaphore_signal(
-            barrier, inc=1, device_id=(vol, lax.rem(rep + step, NY)), device_id_type=MESH
+            barrier, inc=1, device_id=(vol, ys[step]), device_id_type=MESH
         )
         greeted += 1
-    for step in range(1, NP):
-        pl.semaphore_signal(barrier, inc=1, device_id=p_peer(step), device_id_type=MESH)
+    for peer in p_peers:
+        pl.semaphore_signal(barrier, inc=1, device_id=(peer, rep), device_id_type=MESH)
         greeted += 1
 
-    for load in loads:
+    loads[0].wait()
+    w_stem2 = block_diagonal(stem_ref[...])
+    loads[1].wait()
+    loads[2].wait()
+    w_mix2 = block_diagonal(mix_ref[...])
+    hid_sum = mix_sum = jnp.zeros((SLOTS, 2 * C), F32)
+    tall = (CHUNK // SLOTS, SLOTS, 2 * C)
+    for first in range(0, ROWS, CHUNK):
+        for pair in range(first // SLOTS, (first + CHUNK) // SLOTS):
+            x_s[pair * SLOTS:(pair + 1) * SLOTS, :] = cut_ref[:, pair * 128:(pair + 1) * 128]
+        rows = slice(first, first + CHUNK)
+        pre1 = dot(x_s[rows, :], w_stem2)
+        hidden = (pre1 * sigmoid(pre1)).astype(BF16)
+        hid_s[rows, :] = hidden
+        pre2 = dot(hidden, w_mix2)
+        mixed = (pre2 * sigmoid(pre2)).astype(BF16)
+        hid_sum = hid_sum + jnp.sum(hidden.astype(F32).reshape(tall), axis=0)
+        mix_sum = mix_sum + jnp.sum(mixed.astype(F32).reshape(tall), axis=0)
+    hid_sum, mix_sum = fold(hid_sum), fold(mix_sum)
+    for load in loads[3:]:
         load.wait()
     count = count_ref[...]
     cnt_s[p, NEAR] = jnp.broadcast_to(count, (1, 128)).astype(F32)
-    w_stem2 = block_diagonal(stem_ref[...])
-    w_mix2 = block_diagonal(mix_ref[...])
-    for pair in range(PAIRS):
-        x_s[pair * SLOTS:(pair + 1) * SLOTS, :] = cut_ref[:, pair * 128:(pair + 1) * 128]
-
-    def forward(step, sums):
-        hid_sum, mix_sum = sums
-        rows = pl.ds(pl.multiple_of(step * CHUNK, CHUNK), CHUNK)
-        pre1 = dot(x_s[rows, :], w_stem2)
-        sig1 = sigmoid(pre1)
-        hidden = (pre1 * sig1).astype(BF16)
-        slope1_s[rows, :] = sig1 * (1.0 + pre1 * (1.0 - sig1))
-        hid_s[rows, :] = hidden
-        pre2 = dot(hidden, w_mix2)
-        sig2 = sigmoid(pre2)
-        mixed = (pre2 * sig2).astype(BF16)
-        slope2_s[rows, :] = sig2 * (1.0 + pre2 * (1.0 - sig2))
-        hid_sum = hid_sum + jnp.sum(hidden.astype(F32).reshape(CHUNK // SLOTS, SLOTS, 2 * C), axis=0)
-        mix_sum = mix_sum + jnp.sum(mixed.astype(F32).reshape(CHUNK // SLOTS, SLOTS, 2 * C), axis=0)
-        return hid_sum, mix_sum
-
-    start = jnp.zeros((SLOTS, 2 * C), F32)
-    hid_sum, mix_sum = lax.fori_loop(0, ROWS // CHUNK, forward, (start, start))
-    hid_sum, mix_sum = fold(hid_sum), fold(mix_sum)
     w_out = out_ref[...]
-    pooled = ((hid_sum + dot(mix_sum, w_out.astype(F32), HIGHEST)) * (1.0 / PATCHES)).astype(BF16)
+    mix_terms = exact_terms(mix_sum)
+    branch = dot(mix_terms, w_out)
+    branch = branch[:SLOTS] + branch[SLOTS:2 * SLOTS] + branch[2 * SLOTS:]
+    pooled = ((hid_sum + branch) * (1.0 / PATCHES)).astype(BF16)
     raw = dot_nt(pooled, proj_ref[...])
     inv_norm = lax.rsqrt(jnp.sum(raw * raw, axis=1, keepdims=True) + EPS)
     unit = raw * inv_norm
@@ -179,23 +191,11 @@
 
     def share(first, last, kind):
         block = emb_s.at[p, first:last]
-        for step in range(1, NP):
-            send(block, block, kind, p_peer(step))
+        for peer in p_peers:
+            send(block, block, kind, (peer, rep))
 
     def relay(source, target, blocks, kind, towards, ref=emb_s):
         send(ref.at[p, source:source + blocks], ref.at[p, target:target + blocks], kind, z_peer(towards))
-
-    xt_s[...] = x_s[...].T
-    ht_s[...] = hid_s[...].T
-    terms, rest = [], mix_sum
-    for _ in range(3):
-        terms.append(rest.astype(BF16))
-        rest = rest - terms[-1].astype(F32)
-    mix_terms = jnp.concatenate(terms, axis=0).T
-    zero_slots = jnp.zeros((SLOTS, E), BF16)
-    anchors = jnp.concatenate(
-        [jnp.concatenate([embed, zero_slots], axis=1), jnp.concatenate([zero_slots, embed], axis=1)], axis=0
-    )
 
     arrived(emb_s.at[0, 0:4], LINE_NEAR_A)
     relay(5, 9, 2, LINE_FAR_A, -NEAR)
@@ -209,6 +209,26 @@
     arrived(cnt_s.at[0, 0:8], COUNT_NEAR)
     relay(5, 9, 4, COUNT_FAR, -NEAR, cnt_s)
     relay(1, 13, 3, COUNT_FAR, NEAR, cnt_s)
+
+    def slopes(step, carry):
+        rows = pl.ds(pl.multiple_of(step * CHUNK, CHUNK), CHUNK)
+        pre1 = dot(x_s[rows, :], w_stem2)
+        sig1 = sigmoid(pre1)
+        slope1_s[rows, :] = sig1 * (1.0 + pre1 * (1.0 - sig1))
+        pre2 = dot(hid_s[rows, :], w_mix2)
+        sig2 = sigmoid(pre2)
+        slope2_s[rows, :] = sig2 * (1.0 + pre2 * (1.0 - sig2))
+        return carry
+
+    lax.fori_loop(0, ROWS // CHUNK, slopes, 0)
+    xt_s[...] = x_s[...].T
+    ht_s[...] = hid_s[...].T
+    mix_turned = mix_terms.T
+    zero_slots = jnp.zeros((SLOTS, E), BF16)
+    anchors = jnp.concatenate(
+        [jnp.concatenate([embed, zero_slots], axis=1), jnp.concatenate([zero_slots, embed], axis=1)], axis=0
+    )
+
     arrived(emb_s.at[0, 0:4], LINE_FAR_A)
     share(9, 11, PLANE_FAR_A)
     share(14, 16, PLANE_FAR_A)
@@ -216,8 +236,8 @@
     share(11, 14, PLANE_FAR_B)
     arrived(cnt_s.at[0, 0:7], COUNT_FAR)
     count_block = cnt_s.at[p]
-    for step in range(1, NP):
-        send(count_block, count_block, PLANE_COUNT, p_peer(step))
+    for peer in p_peers:
+        send(count_block, count_block, PLANE_COUNT, (peer, rep))
 
     line = emb_s[p].reshape(LINE, 128)
     low = iota((LINE, 128), 1) < E
@@ -259,8 +279,8 @@
     line_sum = fold(jnp.sum(total, axis=0, keepdims=True)) - float(DEAD) - self_sum
     tot_s[p] = jnp.concatenate([line_sum[:, :LINE], line_sum[:, LINE:]], axis=0)
     own_total = tot_s.at[p]
-    for step in range(1, NP):
-        send(own_total, own_total, TOTAL, p_peer(step))
+    for peer in p_peers:
+        send(own_total, own_total, TOTAL, (peer, rep))
 
     every = emb_s[...].reshape(NP * LINE, 128)
     wide = NP * LINE
@@ -334,30 +354,24 @@
     g_proj = dot_tn(d_raw, pooled)
     d_sum = (dot(d_raw, proj_ref[...]) * (1.0 / PATCHES)).astype(BF16)
     d_sum32 = d_sum.astype(F32)
-    g_out = dot(mix_terms, jnp.concatenate([d_sum] * 3, axis=0))
+    g_out = dot(mix_turned, jnp.concatenate([d_sum] * 3, axis=0))
     d_mixed = twice(dot_nt(d_sum, w_out))
     d_spread = twice(d_sum32)
 
-    def scatter(first):
-        def one(step, carry):
-            to = first + lax.rem(q + step, NQ // 2)
-            send(part_s.at[to], gath_s.at[q], PIECE, q_peer(to))
-            return carry
-
-        inside = (q // (NQ // 2) == first // (NQ // 2))
-
-        @pl.when(inside)
+    def scatter(to):
+        for dy, dx in apart:
+            at = to * (NQ // 2) + ys[dy] * 4 + xs[dx]
+            send(part_s.at[at], gath_s.at[piece], PIECE, (plane[dx] + to, ys[dy]))
+
+        @pl.when(core != to)
         def _():
-            lax.fori_loop(1, NQ // 2, one, 0)
-
-        @pl.when(jnp.logical_not(inside))
-        def _():
-            lax.fori_loop(0, NQ // 2, one, 0)
+            at = to * (NQ // 2) + rep * 4 + x
+            send(part_s.at[at], gath_s.at[piece], PIECE, (plane[0] + to, rep))
 
     for tile in range(NQ // 2):
         part_s[16 + tile, 0:8, :] = g_out[tile * 8:(tile + 1) * 8]
         part_s[16 + tile, 8:12, :] = g_proj[tile * 4:(tile + 1) * 4]
-    scatter(NQ // 2)
+    scatter(1)
 
     g_mix = jnp.zeros((2 * C, 2 * C), F32)
     g_stem = jnp.zeros((2 * VOX, 2 * C), F32)
@@ -376,7 +390,7 @@
         part_s[tile, 8:12, :] = g_stem[tile * 4:(tile + 1) * 4]
 
     scatter(0)
-    gath_s[q] = part_s[q]
+    gath_s[piece] = part_s[piece]
 
     out_sum = jnp.zeros((HALF, 1), F32)
     for half in range(2):
@@ -394,13 +408,13 @@
             if step < NZ // 2 or sign == 1:
                 send(zed_s.at[z], zed_s.at[z], PIECE_Z, z_peer(sign * step))
     arrived(zed_s.at[0:NZ - 1], PIECE_Z)
-    fin_s[q] = jnp.sum(zed_s[...], axis=0)
-
-    def spread(step, carry):
-        send(fin_s.at[q], fin_s.at[q], RESULT, q_peer(lax.rem(q + step, NQ)))
-        return carry
-
-    lax.fori_loop(1, NQ, spread, 0)
+    fin_s[piece] = jnp.sum(zed_s[...], axis=0)
+
+    result = fin_s.at[piece]
+    for dy, dx in apart:
+        for to in range(2):
+            send(result, result, RESULT, (plane[dx] + to, ys[dy]))
+    send(result, result, RESULT, (plane[0] + mate, rep))
     arrived(fin_s.at[0:NQ - 1], RESULT)
 
     def normal(g):

time: 55.7 us -> 54 us (0.969)
  Pallas kernels: 54.3 us -> 52.5 us
    pallas_call x1, Pallas kernels: 52.7 us -> 50.9 us  [on_device(): pl.pallas_call(kernel, out_shape=(jax.ShapeDtypeStruct((384, 128), F32),...]
where the time goes in v4:
time: 54 us; the launch traced here: 53.8 us
  Pallas kernels  52.5 us (97%)
  between operations  1.29 us (2%)
    pallas_call x1, Pallas kernels, on_device(): pl.pallas_call(kernel, out_shape=(jax.ShapeDtypeStruct((384, 128), F32),...  50.9 us
    pallas_call x1, Pallas kernels, on_device(): pl.pallas_call(store, out_shape=(jax.ShapeDtypeStruct((VOX, C), F32), jax...  1.61 us

profile of v4, /device:TPU:1, one launch (start us, length us, event | category | flops | bytes accessed | tf_op | source)
XLA Modules:
  0.0 53.8 jit_solution(11451682047119887369)
XLA Ops:
  1.3 50.9 %shard_map.110 = (f32[384,128]{1,0:T(8,128)}, f32[1,16]{1,0:T(1,128)}) custom-call(bf16[32,4096]{1,0:T(8,128)(2,1)} %bitcast.4, s32[1,1]{1,0:T(1,128)S(6)} %copy.12.count_hbm, s32[1,2048]{1,0:T(1,128)} %partner_hbm.1, bf16[64,128]{1,0:T(8,128)(2,1)} %stem_hbm.1, bf16[128,128]{1,0:T(8,128)(2,1)} %mix_hbm.1, bf16[128,128]{1,0:T(8,128)(2,1)} %out_hbm.1, ...), custom_call_target="tpu_custom_call" | custom-call | tf_op jit(solution)/shard_map/pallas_call | solution.py:450
  52.2 1.6 %shard_map.111 = (f32[64,128]{1,0:T(8,128)}, f32[128,128]{1,0:T(8,128)}, f32[128,128]{1,0:T(8,128)}, f32[64,128]{1,0:T(8,128)}, f32[1,16]{1,0:T(1,128)}) custom-call(f32[384,128]{1,0:T(8,128)} %get-tuple-element.12.up_ref, f32[1,16]{1,0:T(1,128)} %get-tuple-element.13.loss_ref), custom_call_target="tpu_custom_call" | custom-call | tf_op jit(solution)/shard_map/pallas_call | solution.py:484

commit v5 on v4

--- a/solution.py
+++ b/solution.py
@@ -436,12 +436,18 @@
         sent(ref, kind)
 
 
-def store(up_ref, loss_ref, stem_ref, mix_ref, out_ref, proj_ref, out_loss_ref):
-    stem_ref[...] = up_ref[0:64]
-    mix_ref[...] = up_ref[64:192]
-    out_ref[...] = up_ref[192:320]
-    proj_ref[...] = up_ref[320:384]
-    out_loss_ref[...] = loss_ref[...]
+def store(up_ref, loss_ref, stem_hbm, mix_hbm, out_hbm, proj_hbm, loss_hbm, sem):
+    copies = [
+        pltpu.make_async_copy(source, target, sem.at[number])
+        for number, (source, target) in enumerate([
+            (up_ref.at[64:192], mix_hbm), (up_ref.at[192:320], out_hbm), (up_ref.at[0:64], stem_hbm),
+            (up_ref.at[320:384], proj_hbm), (loss_ref, loss_hbm),
+        ])
+    ]
+    for copy in copies:
+        copy.start()
+    for copy in copies:
+        copy.wait()
 
 
 def on_device(cutouts, counts, partner, w_stem, w_mix, w_out, w_proj):
@@ -478,9 +484,9 @@
             pltpu.SemaphoreType.DMA((KINDS,)),
         ],
         compiler_params=pltpu.CompilerParams(
-            collective_id=0, has_side_effects=True, vmem_limit_bytes=56 * 1024 * 1024
+            collective_id=0, has_side_effects=True, vmem_limit_bytes=50000 * 1024
         ),
-    )(cutouts[0], counts, partner, w_stem, w_mix, w_out, w_proj.T)
+    )(*[v if v is counts else pltpu.with_memory_space_constraint(v, pltpu.HBM) for v in (cutouts[0], counts, partner, w_stem, w_mix, w_out, w_proj.T)])
     outs = pl.pallas_call(
         store,
         out_shape=(
@@ -490,8 +496,10 @@
             jax.ShapeDtypeStruct((E, C), F32),
             jax.ShapeDtypeStruct((1, HALF), F32),
         ),
-        in_specs=[vmem] * 2,
-        out_specs=(vmem,) * 5,
+        in_specs=[pl.BlockSpec(memory_space=pl.ANY)] * 2,
+        out_specs=(hbm,) * 5,
+        scratch_shapes=[pltpu.SemaphoreType.DMA((5,))],
+        compiler_params=pltpu.CompilerParams(vmem_limit_bytes=4 * 1024 * 1024),
     )(updates, loss)
     return outs[:3] + (outs[3].T, outs[4][None])
 

time: 54 us -> 52.5 us (0.972)
  Pallas kernels: 52.5 us -> 51 us
    pallas_call x1, Pallas kernels: 1.61 us -> 0.72 us  [on_device(): pl.pallas_call(store, out_shape=(jax.ShapeDtypeStruct((VOX, C), F32), jax...]
    pallas_call x1, Pallas kernels: 50.9 us -> 50.2 us  [on_device(): pl.pallas_call(kernel, out_shape=(jax.ShapeDtypeStruct((384, 128), F32),...]
where the time goes in v5:
time: 52.5 us; the launch traced here: 52.3 us
  Pallas kernels  51 us (97%)
  between operations  1.29 us (2%)
    pallas_call x1, Pallas kernels, on_device(): pl.pallas_call(kernel, out_shape=(jax.ShapeDtypeStruct((384, 128), F32),...  50.2 us

profile of v5, /device:TPU:1, one launch (start us, length us, event | category | flops | bytes accessed | tf_op | source)
XLA Modules:
  0.0 52.3 jit_solution(14471813753169065747)
XLA Ops:
  1.3 50.2 %shard_map.110 = (f32[384,128]{1,0:T(8,128)S(1)}, f32[1,16]{1,0:T(1,128)S(1)}) custom-call(bf16[32,4096]{1,0:T(8,128)(2,1)} %bitcast.4, s32[1,1]{1,0:T(1,128)S(6)} %copy.12.count_hbm, s32[1,2048]{1,0:T(1,128)} %partner_hbm.1, bf16[64,128]{1,0:T(8,128)(2,1)} %stem_hbm.1, bf16[128,128]{1,0:T(8,128)(2,1)} %mix_hbm.1, bf16[128,128]{1,0:T(8,128)(2,1)} %out_hbm.1, ...), custom_call_target="tpu_custom_call" | custom-call | tf_op jit(solution)/shard_map/pallas_call | solution.py:456
  51.5 0.7 %shard_map.111 = (f32[64,128]{1,0:T(8,128)}, f32[128,128]{1,0:T(8,128)}, f32[128,128]{1,0:T(8,128)}, f32[64,128]{1,0:T(8,128)}, f32[1,16]{1,0:T(1,128)}) custom-call(f32[384,128]{1,0:T(8,128)S(1)} %get-tuple-element.12.up_ref, f32[1,16]{1,0:T(1,128)S(1)} %get-tuple-element.13.loss_ref), custom_call_target="tpu_custom_call" | custom-call | tf_op jit(solution)/shard_map/pallas_call | solution.py:490

commit v6 on v5

--- a/solution.py
+++ b/solution.py
@@ -49,9 +49,8 @@
 
 
 def sigmoid(v):
-    d = 1.0 + jnp.exp(jnp.minimum(-v, 80.0))
+    d = 1.0 + jnp.exp2(jnp.minimum(v * -LOG2E, 80.0 * LOG2E))
     r = pl.reciprocal(d, approx=True)
-    r = r * (2.0 - d * r)
     return r * (2.0 - d * r)
 
 

time: 52.5 us -> 52.3 us (level)
  no operation moved by 1% of the time
where the time goes in v6:
time: 52.3 us; the launch traced here: 52.1 us
  Pallas kernels  50.8 us (97%)
  between operations  1.29 us (2%)
    pallas_call x1, Pallas kernels, on_device(): pl.pallas_call(kernel, out_shape=(jax.ShapeDtypeStruct((384, 128), F32),...  50.1 us

profile of v6, /device:TPU:1, one launch (start us, length us, event | category | flops | bytes accessed | tf_op | source)
XLA Modules:
  0.0 52.1 jit_solution(9548561910169135548)
XLA Ops:
  1.3 50.1 %shard_map.110 = (f32[384,128]{1,0:T(8,128)S(1)}, f32[1,16]{1,0:T(1,128)S(1)}) custom-call(bf16[32,4096]{1,0:T(8,128)(2,1)} %bitcast.4, s32[1,1]{1,0:T(1,128)S(6)} %copy.12.count_hbm, s32[1,2048]{1,0:T(1,128)} %partner_hbm.1, bf16[64,128]{1,0:T(8,128)(2,1)} %stem_hbm.1, bf16[128,128]{1,0:T(8,128)(2,1)} %mix_hbm.1, bf16[128,128]{1,0:T(8,128)(2,1)} %out_hbm.1, ...), custom_call_target="tpu_custom_call" | custom-call | tf_op jit(solution)/shard_map/pallas_call | solution.py:455
  51.3 0.7 %shard_map.111 = (f32[64,128]{1,0:T(8,128)}, f32[128,128]{1,0:T(8,128)}, f32[128,128]{1,0:T(8,128)}, f32[64,128]{1,0:T(8,128)}, f32[1,16]{1,0:T(1,128)}) custom-call(f32[384,128]{1,0:T(8,128)S(1)} %get-tuple-element.12.up_ref, f32[1,16]{1,0:T(1,128)S(1)} %get-tuple-element.13.loss_ref), custom_call_target="tpu_custom_call" | custom-call | tf_op jit(solution)/shard_map/pallas_call | solution.py:489

commit v7 on v6

--- a/solution.py
+++ b/solution.py
@@ -357,38 +357,42 @@
     d_mixed = twice(dot_nt(d_sum, w_out))
     d_spread = twice(d_sum32)
 
-    def scatter(to):
+    def scatter(to, first, last):
         for dy, dx in apart:
             at = to * (NQ // 2) + ys[dy] * 4 + xs[dx]
-            send(part_s.at[at], gath_s.at[piece], PIECE, (plane[dx] + to, ys[dy]))
+            send(part_s.at[at, first:last], gath_s.at[piece, first:last], PIECE, (plane[dx] + to, ys[dy]))
 
         @pl.when(core != to)
         def _():
             at = to * (NQ // 2) + rep * 4 + x
-            send(part_s.at[at], gath_s.at[piece], PIECE, (plane[0] + to, rep))
+            send(part_s.at[at, first:last], gath_s.at[piece, first:last], PIECE, (plane[0] + to, rep))
 
     for tile in range(NQ // 2):
         part_s[16 + tile, 0:8, :] = g_out[tile * 8:(tile + 1) * 8]
         part_s[16 + tile, 8:12, :] = g_proj[tile * 4:(tile + 1) * 4]
-    scatter(1)
+    scatter(1, 0, 12)
 
     g_mix = jnp.zeros((2 * C, 2 * C), F32)
     g_stem = jnp.zeros((2 * VOX, 2 * C), F32)
+    shape = (CHUNK // SLOTS, SLOTS, 2 * C)
+    d_pre2 = []
     for step in range(ROWS // CHUNK):
         rows = slice(step * CHUNK, (step + 1) * CHUNK)
-        shape = (CHUNK // SLOTS, SLOTS, 2 * C)
-        d_pre2 = (slope2_s[rows, :].reshape(shape) * d_mixed[None]).reshape(CHUNK, 2 * C).astype(BF16)
-        g_mix = g_mix + dot(ht_s[:, rows], d_pre2)
-        d_hid = (dot_nt(d_pre2, w_mix2).reshape(shape) + d_spread[None]).reshape(CHUNK, 2 * C)
+        d_pre2.append((slope2_s[rows, :].reshape(shape) * d_mixed[None]).reshape(CHUNK, 2 * C).astype(BF16))
+        g_mix = g_mix + dot(ht_s[:, rows], d_pre2[step])
+    g_mix = g_mix[:C, :C] + g_mix[C:, C:]
+    for tile in range(NQ // 2):
+        part_s[tile, 0:8, :] = g_mix[tile * 8:(tile + 1) * 8]
+    scatter(0, 0, 8)
+    for step in range(ROWS // CHUNK):
+        rows = slice(step * CHUNK, (step + 1) * CHUNK)
+        d_hid = (dot_nt(d_pre2[step], w_mix2).reshape(shape) + d_spread[None]).reshape(CHUNK, 2 * C)
         d_pre1 = (d_hid * slope1_s[rows, :]).astype(BF16)
         g_stem = g_stem + dot(xt_s[:, rows], d_pre1)
-    g_mix = g_mix[:C, :C] + g_mix[C:, C:]
     g_stem = g_stem[:VOX, :C] + g_stem[VOX:, C:]
     for tile in range(NQ // 2):
-        part_s[tile, 0:8, :] = g_mix[tile * 8:(tile + 1) * 8]
         part_s[tile, 8:12, :] = g_stem[tile * 4:(tile + 1) * 4]
-
-    scatter(0)
+    scatter(0, 8, 12)
     gath_s[piece] = part_s[piece]
 
     out_sum = jnp.zeros((HALF, 1), F32)

time: 52.3 us -> 52.4 us (level)
  no operation moved by 1% of the time
where the time goes in v7:
time: 52.4 us; the launch traced here: 52.2 us
  Pallas kernels  50.9 us (97%)
  between operations  1.29 us (2%)
    pallas_call x1, Pallas kernels, on_device(): pl.pallas_call(kernel, out_shape=(jax.ShapeDtypeStruct((384, 128), F32),...  50.2 us

profile of v7, /device:TPU:1, one launch (start us, length us, event | category | flops | bytes accessed | tf_op | source)
XLA Modules:
  0.0 52.2 jit_solution(15642624935941996792)
XLA Ops:
  1.3 50.2 %shard_map.110 = (f32[384,128]{1,0:T(8,128)S(1)}, f32[1,16]{1,0:T(1,128)S(1)}) custom-call(bf16[32,4096]{1,0:T(8,128)(2,1)} %bitcast.4, s32[1,1]{1,0:T(1,128)S(6)} %copy.12.count_hbm, s32[1,2048]{1,0:T(1,128)} %partner_hbm.1, bf16[64,128]{1,0:T(8,128)(2,1)} %stem_hbm.1, bf16[128,128]{1,0:T(8,128)(2,1)} %mix_hbm.1, bf16[128,128]{1,0:T(8,128)(2,1)} %out_hbm.1, ...), custom_call_target="tpu_custom_call" | custom-call | tf_op jit(solution)/shard_map/pallas_call | solution.py:459
  51.4 0.7 %shard_map.111 = (f32[64,128]{1,0:T(8,128)}, f32[128,128]{1,0:T(8,128)}, f32[128,128]{1,0:T(8,128)}, f32[64,128]{1,0:T(8,128)}, f32[1,16]{1,0:T(1,128)}) custom-call(f32[384,128]{1,0:T(8,128)S(1)} %get-tuple-element.12.up_ref, f32[1,16]{1,0:T(1,128)S(1)} %get-tuple-element.13.loss_ref), custom_call_target="tpu_custom_call" | custom-call | tf_op jit(solution)/shard_map/pallas_call | solution.py:493
